TPU v7x, 512 devices: a whole 4x4x16 slice. The times are simulated.
512 devices in a mesh: lat: 64 (over z_hi, y, x, core), lon: 8 (over z_lo).
Axes of the slice: x: 4, y: 4, z: 16 (z_hi: 2, z_lo: 8; z = z_hi * 8 + z_lo), core: 2. Of those that a mesh axis runs over, the one named last changes fastest.
Arguments:
- tokens: bfloat16 [384, 384, 512], P('lat', 'lon')
- cotangent: bfloat16 [384, 384, 512], P('lat', 'lon'), may hold values from -6 to 6
- qkv_weight: bfloat16 [512, 1536], P('lat', 'lon')
- band_rows: int32 [64], replicated, may hold values from 4 to 6, as said below
Outputs:
- token_grad: bfloat16 [384, 384, 512], P('lat', 'lon')
- weight_gradient: float32 [512, 1536], P('lat', 'lon')
Inputs may be any that keep to these rules, and one draw needn't show every extreme that they name: `band_rows`: some band is full.
All inputs are finite; a program needn't handle non-finite values.
Results may differ from a plain program's by a relative error of at most 0.017.
Values may be sent and summed in bfloat16 or wider, within the bound.
A program may use at most 64 MiB of HBM per device.

v0:
```python
import jax
import jax.numpy as jnp
from jax import lax
from jax.sharding import PartitionSpec as P

HEADS = 16
HEAD_DIM = 32
WIN_ROWS = 6
WIN_COLS = 12


epsilon = 1e-05


def shifted(array, axis, by):
    length = lax.axis_size(axis)
    pairs = [(i, i + by) for i in range(length) if 0 <= i + by < length]
    return lax.ppermute(array, axis, pairs)


def from_behind(block, axis, distance):
    devices = range(lax.axis_size(axis))
    route = [((i - distance) % len(devices), i) for i in devices]
    return lax.ppermute(block, axis, route)


def to_windows(tensor):
    row_count, col_count, feature_count = tensor.shape
    head_width = feature_count // HEADS
    tensor = tensor.reshape(
        row_count // WIN_ROWS, WIN_ROWS, col_count // WIN_COLS, WIN_COLS, HEADS, head_width
    )
    tensor = tensor.transpose(0, 2, 4, 1, 3, 5)
    return tensor.reshape(-1, HEADS, WIN_ROWS * WIN_COLS, head_width)


def from_windows(tensor, row_count, col_count):
    head_width = tensor.shape[-1]
    tensor = tensor.reshape(
        row_count // WIN_ROWS, col_count // WIN_COLS, HEADS, WIN_ROWS, WIN_COLS, head_width
    )
    tensor = tensor.transpose(0, 3, 1, 4, 2, 5)
    return tensor.reshape(row_count, col_count, HEADS * head_width)


def key_mask(valid_rows, col_count):
    row_count = valid_rows.shape[0]
    spread = jnp.broadcast_to(
        valid_rows.reshape(row_count // WIN_ROWS, 1, WIN_ROWS, 1),
        (row_count // WIN_ROWS, col_count // WIN_COLS, WIN_ROWS, WIN_COLS),
    )
    return spread.reshape(-1, WIN_ROWS * WIN_COLS)


def product(form, left, right):
    return jnp.einsum(form, left, right, preferred_element_type=jnp.float32)


def normalize(block):
    values = block.astype(jnp.float32)
    center = values - jnp.mean(values, axis=-1, keepdims=True)
    inverse = lax.rsqrt(jnp.mean(center * center, axis=-1, keepdims=True) + epsilon)
    return (center * inverse, inverse)


def norm_backward(grad_in, normed, inverse):
    mean_grad = jnp.mean(grad_in, axis=-1, keepdims=True)
    mean_mixed = jnp.mean(grad_in * normed, axis=-1, keepdims=True)
    return inverse * (grad_in - mean_grad - normed * mean_mixed)


def window_backward(qkv_block, grad_block, valid_rows):
    row_count, col_count, triple = qkv_block.shape
    width = triple // 3
    query = to_windows(qkv_block[..., :width])
    keyed = to_windows(qkv_block[..., width : 2 * width])
    valued = to_windows(qkv_block[..., 2 * width :])
    masked_grad = jnp.where(valid_rows[:, None, None], grad_block, jnp.zeros_like(grad_block))
    out_grad = to_windows(masked_grad)
    factor = HEAD_DIM ** (-0.5)
    allowed = key_mask(valid_rows, col_count)
    scores = product("whqd,whkd->whqk", query, keyed) * factor
    scores = jnp.where(allowed[:, None, None, :], scores, -1000000000.0)
    scores = scores - jnp.max(scores, axis=-1, keepdims=True)
    exponent = jnp.exp(scores)
    probs = exponent / jnp.sum(exponent, axis=-1, keepdims=True)
    probs_low = probs.astype(jnp.bfloat16)
    weight_grad = product("whqd,whkd->whqk", out_grad, valued)
    value_grad = product("whqk,whqd->whkd", probs_low, out_grad)
    score_grad = (
        probs * (weight_grad - jnp.sum(probs * weight_grad, axis=-1, keepdims=True)) * factor
    ).astype(jnp.bfloat16)
    query_grad = product("whqk,whkd->whqd", score_grad, keyed)
    key_grad = product("whqk,whqd->whkd", score_grad, query)
    joined = jnp.concatenate(
        [
            from_windows(query_grad, row_count, col_count),
            from_windows(key_grad, row_count, col_count),
            from_windows(value_grad, row_count, col_count),
        ],
        axis=-1,
    )
    return joined.astype(jnp.bfloat16)


def on_device(tokens, cotangent, qkv_weight, band_rows):
    row_count, col_count, feature_count = tokens.shape
    shift_rows = WIN_ROWS // 2
    shift_cols = WIN_COLS // 2
    paired = jnp.concatenate([tokens, cotangent], axis=2)
    arrived = shifted(paired[row_count - shift_rows :], "lat", 1)
    paired = jnp.concatenate([arrived, paired[: row_count - shift_rows]], axis=0)
    arrived = from_behind(paired[:, col_count - shift_cols :], "lon", 1)
    paired = jnp.concatenate([arrived, paired[:, : col_count - shift_cols]], axis=1)
    framed_tokens = paired[..., :feature_count]
    framed_cotangent = paired[..., feature_count:]
    band_index = lax.axis_index("lat")
    own_count = band_rows[band_index]
    previous = jnp.where(band_index > 0, band_rows[jnp.maximum(band_index - 1, 0)], 0)
    local_rows = jnp.arange(row_count, dtype=jnp.int32)
    framed_valid = jnp.where(
        local_rows < shift_rows,
        local_rows + row_count - shift_rows < previous,
        local_rows - shift_rows < own_count,
    )
    normed, inverse = normalize(framed_tokens)
    hidden = normed.astype(jnp.bfloat16).reshape(-1, feature_count)
    columns = lax.all_gather(qkv_weight, "lon", axis=1, tiled=True)
    whole_weight = lax.all_gather(columns, "lat", axis=0, tiled=True)
    qkv = jnp.dot(hidden, whole_weight, preferred_element_type=jnp.float32)
    qkv_grad = window_backward(
        qkv.astype(jnp.bfloat16).reshape(row_count, col_count, -1), framed_cotangent, framed_valid
    ).reshape(-1, 3 * feature_count)
    grad_part = lax.psum_scatter(
        jnp.dot(hidden.T, qkv_grad, preferred_element_type=jnp.float32),
        "lat",
        scatter_dimension=0,
        tiled=True,
    )
    weight_gradient = lax.psum_scatter(
        grad_part.astype(jnp.bfloat16), "lon", scatter_dimension=1, tiled=True
    ).astype(jnp.float32)
    hidden_grad = jnp.dot(qkv_grad, whole_weight.T, preferred_element_type=jnp.float32)
    hidden_grad = hidden_grad.reshape(row_count, col_count, feature_count)
    frame_grad = norm_backward(hidden_grad, normed, inverse).astype(jnp.bfloat16)
    arrived = from_behind(frame_grad[:, :shift_cols], "lon", -1)
    frame_grad = jnp.concatenate([frame_grad[:, shift_cols:], arrived], axis=1)
    arrived = shifted(frame_grad[:shift_rows], "lat", -1)
    frame_grad = jnp.concatenate([frame_grad[shift_rows:], arrived], axis=0)
    token_grad = (cotangent.astype(jnp.float32) + frame_grad.astype(jnp.float32)).astype(
        jnp.bfloat16
    )
    return (token_grad, weight_gradient)


def solution(mesh):
    return jax.shard_map(
        on_device,
        mesh=mesh,
        in_specs=(P("lat", "lon", None), P("lat", "lon", None), P("lat", "lon"), P()),
        out_specs=(P("lat", "lon", None), P("lat", "lon")),
        check_vma=False,
    )
```

profile of v0, /device:TPU:6, one launch (start us, length us, event | category | flops | bytes accessed | tf_op | source)
XLA Modules:
  0.0 470.0 jit_solution(1482922452450199518)
XLA Ops:
  7.2 48.9 %all-gather = bf16[8,192,8]{1,2,0:T(8,128)(2,1)S(1)} all-gather(bf16[1,192,8]{1,2,0:T(8,128)(2,1)} %bitcast.69), channel_id=1, replica_groups=mesh['lat'=64,'lon'=8] {'lon'}, dimensions={0}, use_global_device_ids=true | all-gather | bytes 27648 | tf_op jit(solution)/shard_map/all_gather | solution.py:128
  56.9 1.0 constant_dynamic-update-slice_fusion.1
  57.9 1.0 constant_dynamic-update-slice_fusion
  59.0 1.9 collective-permute-start
  62.2 4.8 %collective-permute-done = bf16[3,48,1024]{2,1,0:T(8,128)(2,1)S(1)} collective-permute-done((bf16[3,48,1024]{2,1,0:T(8,128)(2,1)S(1)}, bf16[3,48,1024]{2,1,0:T(8,128)(2,1)S(1)}, u32[]{:S(2)}, u32[]{:S(2)}) %collective-permute-start) | collective-permute-done | bytes 294944 | tf_op jit(solution)/shard_map/ppermute | solution.py:18
  67.1 3.8 collective-permute-start.1
  71.7 8.6 %collective-permute-done.1 = bf16[6,6,1024]{2,1,0:T(8,128)(2,1)S(1)} collective-permute-done((bf16[6,6,1024]{2,1,0:T(8,128)(2,1)S(1)}, bf16[6,6,1024]{2,1,0:T(8,128)(2,1)S(1)}, u32[]{:S(2)}, u32[]{:S(2)}) %collective-permute-start.1) | collective-permute-done | bytes 73760 | tf_op jit(solution)/shard_map/ppermute | solution.py:24
  81.4 1.1 copy.63
  83.0 81.4 %all-gather.3.cloned.1.call-done = bf16[512,1536]{1,0:T(8,128)(2,1)} async-done(((bf16[8,1536]{1,0:T(8,128)(2,1)}), bf16[512,1536]{1,0:T(8,128)(2,1)}) %all-gather.3.cloned.1.call-update) | async-done | bytes 1572880 | tf_op jit(solution)/shard_map/all_gather | solution.py:129
  164.4 2.0 convolution_convert_fusion
  168.2 1.7 copy.59
  170.0 1.8 reshape.124
  171.8 1.2 copy.62
  173.9 1.7 copy.60
  175.6 2.0 fusion.20
  177.6 3.9 fusion.52
  181.6 3.2 convolution_convert_fusion.1
  184.8 3.3 fusion.17
  188.1 4.2 fusion.14
  192.2 1.9 copy.67
  194.4 1.1 concatenate.30
  196.3 1.2 copy.71
  197.7 1.1 concatenate.31
  198.8 1.9 copy.75
  201.0 1.1 concatenate.32
  203.7 3.9 convolution_bitcast_fusion
  207.6 1.1 copy-done.4
  210.2 2.3 collective-permute-start.2
  212.6 3.6 collective-permute-done.2
  216.3 1.9 collective-permute-start.3
  218.2 185.6 %reduce-scatter.5.cloned.1.call-done = f32[8,1536]{1,0:T(8,128)} async-done(((f32[512,1536]{1,0:T(8,128)}), f32[8,1536]{1,0:T(8,128)}) %reduce-scatter.5.cloned.1.call-update) | async-done | bytes 49168 | tf_op jit(solution)/shard_map/reduce_scatter | solution.py:134
  406.3 55.7 %reduce-scatter.7.cloned.1.call-done = bf16[192,8]{1,0:T(8,128)(2,1)} async-done(((bf16[1536,8]{1,0:T(8,128)(2,1)}), bf16[192,8]{1,0:T(8,128)(2,1)}) %reduce-scatter.7.cloned.1.call-update) | async-done | bytes 3088
  (59 shorter events, 15.1 us)
Async XLA Ops:
  7.2 53.8 %copy-start.5 = (s32[64]{0:T(128)S(1)}, s32[64]{0:T(128)}, u32[]{:S(2)}) copy-start(s32[64]{0:T(128)} %param.7) | copy-start | bytes 772
  7.2 157.2 %all-gather.3.cloned.1.call-start = ((), (), s32[]{:S(2)}) async-start(), calls=%async_computation.2 | async-start | bytes 1597440 | tf_op jit(solution)/shard_map/all_gather | solution.py:129
  56.9 346.9 %reduce-scatter.5.cloned.1.call-start = ((), (), s32[]{:S(2)}) async-start(), calls=%async_computation.3 | async-start | bytes 3194880 | tf_op jit(solution)/shard_map/reduce_scatter | solution.py:134
  59.0 8.0 %collective-permute-start = (bf16[3,48,1024]{2,1,0:T(8,128)(2,1)S(1)}, bf16[3,48,1024]{2,1,0:T(8,128)(2,1)S(1)}, u32[]{:S(2)}, u32[]{:S(2)}) collective-permute-start(bf16[3,48,1024]{2,1,0:T(8,128)(2,1)S(1)} %get-tuple-element.7), channel_id=1, source_target_pairs={{0,8},{8,16},{16,24},{24,32},{32,40},{40,48},{48,56},{56,64},{64,7... | collective-permute-start | bytes 884744 | tf_op jit(solution)/shard_map/ppermute | solution.py:18
  67.1 13.2 %collective-permute-start.1 = (bf16[6,6,1024]{2,1,0:T(8,128)(2,1)S(1)}, bf16[6,6,1024]{2,1,0:T(8,128)(2,1)S(1)}, u32[]{:S(2)}, u32[]{:S(2)}) collective-permute-start(bf16[6,6,1024]{2,1,0:T(8,128)(2,1)S(1)} %pad_maximum_fusion.2), channel_id=1, source_target_pairs={{7,0},{0,1},{1,2},{2,3},{3,4},{4,5},{5,6},{6,7},{15,8},{8,9},{9,10... | collective-permute-start | bytes 221192 | tf_op jit(solution)/shard_map/ppermute | solution.py:24
  83.0 84.4 %copy-start.2 = (bf16[6,48,512]{2,1,0:T(8,128)(2,1)}, bf16[6,48,512]{2,1,0:T(8,128)(2,1)S(1)}, u32[]{:S(2)}) copy-start(bf16[6,48,512]{2,1,0:T(8,128)(2,1)S(1)} %fusion.32) | copy-start | bytes 884740
  170.0 3.1 copy-start.1
  200.8 2.9 copy-start.3
  207.5 1.2 copy-start.4
  207.5 1.7 copy-start.6
  207.6 254.4 %reduce-scatter.7.cloned.1.call-start = ((), (), s32[]{:S(2)}) async-start(), calls=%async_computation.4 | async-start | bytes 442368
  210.0 195.6 %copy-start = (bf16[6,48,512]{2,1,0:T(8,128)(2,1)S(1)}, bf16[6,48,512]{2,1,0:T(8,128)(2,1)}, u32[]{:S(2)}) copy-start(bf16[6,48,512]{2,1,0:T(8,128)(2,1)} %param.5) | copy-start | bytes 884740
  210.2 6.0 %collective-permute-start.2 = (bf16[6,6,512]{2,1,0:T(8,128)(2,1)S(1)}, bf16[6,6,512]{2,1,0:T(8,128)(2,1)S(1)}, u32[]{:S(2)}, u32[]{:S(2)}) collective-permute-start(bf16[6,6,512]{2,1,0:T(8,128)(2,1)S(1)} %slice.60), channel_id=1, source_target_pairs={{1,0},{2,1},{3,2},{4,3},{5,4},{6,5},{7,6},{0,7},{9,8},{10,9},{11,1... | collective-permute-start | bytes 110600 | tf_op jit(solution)/shard_map/ppermute | solution.py:24
  216.3 189.3 %collective-permute-start.3 = (bf16[3,48,512]{2,1,0:T(8,128)(2,1)S(1)}, bf16[3,48,512]{2,1,0:T(8,128)(2,1)S(1)}, u32[]{:S(2)}, u32[]{:S(2)}) collective-permute-start(bf16[3,48,512]{2,1,0:T(8,128)(2,1)S(1)} %get-tuple-element.10), channel_id=1, source_target_pairs={{8,0},{16,8},{24,16},{32,24},{40,32},{48,40},{56,48},{64,56},{72,6... | collective-permute-start | bytes 442376 | tf_op jit(solution)/shard_map/ppermute | solution.py:18
Sparse Core Ops, SparseCore 0:
  57.0 107.3 all-gather.2
  207.7 196.0 reduce-scatter.4
  406.8 55.1 reduce-scatter.6
where the time goes:
time: 471 us; the launch traced here: 470 us
  waiting for transfers between devices  340 us (72%)
  blocking collectives  48.9 us (10%)
  local copies, waits for them, and re-layouts  29.4 us (6%)
  matrix products  23.2 us (5%)
  between operations  14.8 us (3%)
  starting transfers between devices  10.1 us (2%)
    reduce_scatter x1, waiting for transfers between devices, on_device(): lax.psum_scatter(jnp.dot(hidden.T, qkv_grad, preferred_element_type=jnp.f...  186 us
    all_gather x1, waiting for transfers between devices, on_device(): whole_weight = lax.all_gather(columns, 'lat', axis=0, tiled=True)  81.4 us
    unnamed x4, waiting for transfers between devices  55.7 us
    all_gather x1, blocking collectives, on_device(): columns = lax.all_gather(qkv_weight, 'lon', axis=1, tiled=True)  48.9 us
    dot_general x4, matrix products, product(): return jnp.einsum(form, left, right, preferred_element_type=jnp.float32)  12.7 us
    ppermute x2, waiting for transfers between devices, from_behind(): return lax.ppermute(block, axis, route)  12.1 us
  transfers between devices with their start and end apart: 7, of which 6 were waited for; matrix products, arithmetic and copies ran while one was open for 2% of the time, Pallas kernels for 0%

commit v1 on v0

v1 whole, which is shorter than its diff:
```python
import functools

import jax
import jax.numpy as jnp
import numpy as np
from jax import lax
from jax.experimental import pallas as pl
from jax.experimental.pallas import tpu as pltpu
from jax.sharding import PartitionSpec as P

MESH = pl.DeviceIdType.MESH
VMEM = pltpu.VMEM
BF16 = jnp.bfloat16
F32 = jnp.float32

WIN_ROWS = 6
WIN_COLS = 12
SHIFT_ROWS = 3
SHIFT_COLS = 6
HEAD_DIM = 32
EPSILON = 1e-05

Z_HI, Y, X, CORES = 2, 4, 4, 2


class Place:
    def __init__(self, lats, lons):
        self.lats, self.lons = lats, lons
        self.planes = Y * X
        self.rings = Z_HI * lons
        self.lat = lax.axis_index("lat")
        self.lon = lax.axis_index("lon")
        self.z_hi = self.lat // (self.planes * CORES)
        self.p = (self.lat % (self.planes * CORES)) // CORES
        self.core = self.lat % CORES
        self.z = self.z_hi * lons + self.lon

    def ring_at(self, z):
        return ((z // self.lons) * self.planes * CORES + self.p * CORES + self.core, z % self.lons)

    def plane_at(self, p):
        return (self.z_hi * self.planes * CORES + p * CORES + self.core, self.lon)

    def ring_index(self, k):
        return (self.z + k) % self.rings

    def plane_index(self, k):
        x = (self.p % X + k % X) % X
        y = (self.p // X + k // X) % Y
        return y * X + x

    def partner(self):
        return (self.lat + 1 - 2 * self.core, self.lon)

    def east(self):
        return (self.lon + 1) % self.lons

    def west(self):
        return (self.lon + self.lons - 1) % self.lons


def remote(src, dst, send, recv, device):
    return pltpu.make_async_remote_copy(
        src_ref=src, dst_ref=dst, send_sem=send, recv_sem=recv, device_id=device, device_id_type=MESH
    )


def enter(place):
    barrier = pltpu.get_barrier_semaphore()

    def signal(device):
        pl.semaphore_signal(barrier, inc=1, device_id=device, device_id_type=MESH)

    @pl.loop(1, place.rings)
    def _(k):
        signal(place.ring_at(place.ring_index(k)))

    @pl.loop(1, place.planes)
    def _(k):
        signal(place.plane_at(place.plane_index(k)))

    signal(place.partner())
    signal((place.lat, place.east()))
    signal((place.lat, place.west()))
    not_first = place.lat > 0
    not_last = place.lat < place.lats - 1

    @pl.when(not_first)
    def _():
        signal((place.lat - 1, place.lon))
        signal((place.lat - 1, place.west()))

    @pl.when(not_last)
    def _():
        signal((place.lat + 1, place.lon))
        signal((place.lat + 1, place.east()))

    count = place.rings + place.planes + 1
    count = count + jnp.where(not_first, 2, 0) + jnp.where(not_last, 2, 0)
    pl.semaphore_wait(barrier, count)


def gather_kernel(
    lats, lons, tok, cot, w, sel, w_out, row_tok, row_cot, side,
    wide, unit, units, blocks, packed, ring_send, ring_recv, plane_send, plane_recv,
    core_send, core_recv, halo_send, halo_recv,
):
    place = Place(lats, lons)
    half = tok.shape[0] // 2
    features = tok.shape[1]
    columns = w_out.shape[1]
    lane = lax.broadcasted_iota(jnp.int32, (8, 128), 1)

    for part in range(2):
        rows = pl.ds(part * half, half)
        packed[part] = (
            jnp.dot(sel[0], tok[rows], preferred_element_type=F32)
            + jnp.dot(sel[1], cot[rows], preferred_element_type=F32)
        ).astype(BF16)
    wide[...] = jnp.zeros_like(wide)
    wide[:, 0 : w.shape[1]] = w[...].astype(F32)
    unit[...] = jnp.concatenate([wide[:, 0:128], wide[:, 128:256]], axis=0).astype(BF16)

    enter(place)

    def ring_copy(k):
        return remote(
            unit, units.at[place.z], ring_send.at[k], ring_recv.at[place.z],
            place.ring_at(place.ring_index(k)),
        )

    def ring_arrival(k):
        z = place.ring_index(k)
        return remote(unit, units.at[z], ring_send.at[k], ring_recv.at[z], place.ring_at(z))

    @pl.loop(1, place.rings)
    def _(k):
        ring_copy(k).start()

    not_first = place.lat > 0
    not_last = place.lat < lats - 1
    south = (place.lat + 1, place.lon)
    side_copy = remote(packed.at[0], side.at[0], halo_send.at[0], halo_recv.at[0], (place.lat, place.east()))
    diag_copy = remote(
        packed.at[1], side.at[1], halo_send.at[1], halo_recv.at[1], (place.lat + 1, place.east())
    )
    tok_copy = remote(tok.at[pl.ds(half, half)], row_tok, halo_send.at[2], halo_recv.at[2], south)
    cot_copy = remote(cot.at[pl.ds(half, half)], row_cot, halo_send.at[3], halo_recv.at[3], south)
    side_copy.start()

    @pl.when(not_last)
    def _():
        diag_copy.start()
        tok_copy.start()
        cot_copy.start()

    @pl.when(jnp.logical_not(not_first))
    def _():
        side[1] = jnp.zeros(side.shape[1:], BF16)
        row_tok[...] = jnp.zeros_like(row_tok)
        row_cot[...] = jnp.zeros_like(row_cot)

    units[place.z] = unit[...]

    @pl.loop(1, place.rings)
    def _(k):
        ring_arrival(k).wait_recv()

    own = blocks.at[place.core, place.p]
    for pair in range(lons // 2):
        tiles = [[], [], []]
        for z_hi in range(Z_HI):
            even = units[z_hi * lons + 2 * pair].astype(F32)
            odd = units[z_hi * lons + 2 * pair + 1].astype(F32)
            turned_top = pltpu.roll(odd[0:8], 64, 1)
            turned_low = pltpu.roll(odd[8:16], 64, 1)
            tiles[0].append(even[0:8])
            tiles[1].append(jnp.where(lane < 64, even[8:16], turned_top))
            tiles[2].append(jnp.where(lane < 64, turned_top, turned_low))
        for j in range(3):
            own[:, pl.ds(pair * 384 + j * 128, 128)] = jnp.concatenate(tiles[j], axis=0).astype(BF16)

    def plane_copy(k):
        return remote(
            own, own, plane_send.at[k], plane_recv.at[place.p], place.plane_at(place.plane_index(k))
        )

    def plane_arrival(k):
        p = place.plane_index(k)
        block = blocks.at[place.core, p]
        return remote(block, block, plane_send.at[k], plane_recv.at[p], place.plane_at(p))

    def core_copy(p):
        block = blocks.at[place.core, p]
        return remote(block, block, core_send.at[p], core_recv.at[p], place.partner())

    def core_arrival(p):
        block = blocks.at[1 - place.core, p]
        return remote(block, block, core_send.at[p], core_recv.at[p], place.partner())

    @pl.loop(1, place.planes)
    def _(k):
        plane_copy(k).start()

    core_copy(place.p).start()

    @pl.loop(1, place.planes)
    def _(k):
        plane_arrival(k).wait_recv()
        core_copy(place.plane_index(k)).start()

    rows = place.planes * 16

    @pl.loop(0, place.planes)
    def _(k):
        p = place.plane_index(k)
        core_arrival(p).wait_recv()
        first = blocks[0, p].astype(F32)
        second = blocks[1, p].astype(F32)
        for z_hi in range(Z_HI):
            take = slice(z_hi * 8, z_hi * 8 + 8)
            at = pl.multiple_of(z_hi * rows + p * 16, 16)
            w_out[pl.ds(at, 16), :] = jnp.concatenate([first[take], second[take]], axis=0).astype(BF16)

    @pl.when(not_first)
    def _():
        diag_copy.wait_recv()
        tok_copy.wait_recv()
        cot_copy.wait_recv()

    side_copy.wait_recv()
    side_copy.wait_send()

    @pl.when(not_last)
    def _():
        diag_copy.wait_send()
        tok_copy.wait_send()
        cot_copy.wait_send()

    @pl.loop(1, place.rings)
    def _(k):
        ring_copy(k).wait_send()

    @pl.loop(1, place.planes)
    def _(k):
        plane_copy(k).wait_send()

    @pl.loop(0, place.planes)
    def _(k):
        core_copy(k).wait_send()


def gather(tok, cot, w, lats, lons):
    tokens, features = tok.shape
    half = tokens // 2
    cols = half // SHIFT_ROWS
    planes, rings = Y * X, Z_HI * lons
    columns = w.shape[1] * lons
    sel = np.zeros((2, 48, half), np.float32)
    for r in range(SHIFT_ROWS):
        for c in range(SHIFT_COLS):
            sel[0, r * SHIFT_COLS + c, r * cols + cols - SHIFT_COLS + c] = 1
            sel[1, 18 + r * SHIFT_COLS + c, r * cols + cols - SHIFT_COLS + c] = 1
    return pl.pallas_call(
        functools.partial(gather_kernel, lats, lons),
        out_shape=(
            jax.ShapeDtypeStruct((8 * lats, columns), BF16),
            jax.ShapeDtypeStruct((half, features), BF16),
            jax.ShapeDtypeStruct((half, features), BF16),
            jax.ShapeDtypeStruct((2, 48, features), BF16),
        ),
        in_specs=[pl.BlockSpec(memory_space=VMEM)] * 4,
        out_specs=[pl.BlockSpec(memory_space=VMEM)] * 4,
        scratch_shapes=[
            VMEM((8, 256), F32),
            VMEM((16, 128), BF16),
            VMEM((rings, 16, 128), BF16),
            VMEM((CORES, planes, 16, columns), BF16),
            VMEM((2, 48, features), BF16),
            pltpu.SemaphoreType.DMA((rings,)),
            pltpu.SemaphoreType.DMA((rings,)),
            pltpu.SemaphoreType.DMA((planes,)),
            pltpu.SemaphoreType.DMA((planes,)),
            pltpu.SemaphoreType.DMA((planes,)),
            pltpu.SemaphoreType.DMA((planes,)),
            pltpu.SemaphoreType.DMA((4,)),
            pltpu.SemaphoreType.DMA((4,)),
        ],
        compiler_params=pltpu.CompilerParams(
            collective_id=0, has_side_effects=True, vmem_limit_bytes=32 * 2**20
        ),
        name="gather",
    )(tok, cot, w, jnp.asarray(sel, BF16))


def sum_kernel(
    lats, lons, part, back, cot, place_sel, token_grad, weight_grad,
    from_core, sums, from_plane, total, units, from_ring, row_back, side_back,
    core_send, core_recv, plane_send, plane_recv, ring_send, ring_recv, halo_send, halo_recv,
):
    place = Place(lats, lons)
    half = cot.shape[0] // 2
    lane = lax.broadcasted_iota(jnp.int32, (8, 128), 1)
    enter(place)

    def core_copy(p):
        return remote(
            part.at[1 - place.core, p], from_core.at[p], core_send.at[p], core_recv.at[p], place.partner()
        )

    def plane_copy(k):
        p = place.plane_index(k)
        return remote(
            sums.at[p], from_plane.at[place.p], plane_send.at[p], plane_recv.at[place.p], place.plane_at(p)
        )

    def plane_arrival(k):
        p = place.plane_index(k)
        return remote(sums.at[p], from_plane.at[p], plane_send.at[p], plane_recv.at[p], place.plane_at(p))

    def ring_copy(k):
        z = place.ring_index(k)
        return remote(
            units.at[z], from_ring.at[place.z], ring_send.at[z], ring_recv.at[place.z], place.ring_at(z)
        )

    def ring_arrival(k):
        z = place.ring_index(k)
        return remote(units.at[z], from_ring.at[z], ring_send.at[z], ring_recv.at[z], place.ring_at(z))

    @pl.loop(0, place.planes)
    def _(k):
        core_copy(place.plane_index(k + 1)).start()

    not_first = place.lat > 0
    not_last = place.lat < lats - 1
    side_copy = remote(
        back.at[pl.ds(2 * half, 32)], side_back.at[0], halo_send.at[0], halo_recv.at[0],
        (place.lat, place.west()),
    )
    diag_copy = remote(
        back.at[pl.ds(2 * half + 32, 32)], side_back.at[1], halo_send.at[1], halo_recv.at[1],
        (place.lat - 1, place.west()),
    )
    row_copy = remote(
        back.at[pl.ds(half, half)], row_back, halo_send.at[2], halo_recv.at[2], (place.lat - 1, place.lon)
    )

    @pl.when(not_first)
    def _():
        row_copy.start()
        diag_copy.start()

    side_copy.start()

    @pl.when(jnp.logical_not(not_last))
    def _():
        row_back[...] = jnp.zeros_like(row_back)
        side_back[1] = jnp.zeros(side_back.shape[1:], BF16)

    @pl.loop(0, place.planes)
    def _(k):
        p = place.plane_index(k + 1)
        core_copy(p).wait_recv()
        sums[p] = (part[place.core, p].astype(F32) + from_core[p].astype(F32)).astype(BF16)

        @pl.when(k < place.planes - 1)
        def _():
            plane_copy(k + 1).start()

    total[...] = sums[place.p].astype(F32)

    @pl.loop(1, place.planes)
    def _(k):
        plane_arrival(k).wait_recv()
        total[...] += from_plane[place.plane_index(k)].astype(F32)

    for pair in range(lons // 2):
        for z_hi in range(Z_HI):
            tiles = [
                total[pl.ds(z_hi * 8, 8), pl.ds(pair * 384 + j * 128, 128)] for j in range(3)
            ]
            turned = [pltpu.roll(tile, 64, 1) for tile in tiles]
            units[z_hi * lons + 2 * pair] = jnp.concatenate([tiles[0], tiles[1]], axis=0).astype(BF16)
            units[z_hi * lons + 2 * pair + 1] = jnp.concatenate(
                [jnp.where(lane < 64, turned[1], turned[2]), turned[2]], axis=0
            ).astype(BF16)

    @pl.loop(1, place.rings)
    def _(k):
        ring_copy(k).start()

    @pl.when(not_last)
    def _():
        row_copy.wait_recv()
        diag_copy.wait_recv()

    side_copy.wait_recv()
    for part_of in range(2):
        rows = pl.ds(part_of * half, half)
        inner = back[0:half] if part_of == 0 else row_back[...]
        outer = jnp.dot(place_sel[...], side_back[part_of], preferred_element_type=F32)
        token_grad[rows] = (cot[rows].astype(F32) + (inner.astype(F32) + outer)).astype(BF16)

    result = units[place.z].astype(F32)
    from_ring[place.z] = units[place.z]

    @pl.loop(1, place.rings)
    def _(k):
        ring_arrival(k).wait_recv()

    result = from_ring[0].astype(F32)
    for z in range(1, place.rings):
        result = result + from_ring[z].astype(F32)
    weight_grad[:, 0:128] = result[0:8]
    weight_grad[:, 128:192] = result[8:16, 0:64]

    @pl.when(not_first)
    def _():
        row_copy.wait_send()
        diag_copy.wait_send()

    side_copy.wait_send()

    @pl.loop(0, place.planes)
    def _(k):
        core_copy(place.plane_index(k + 1)).wait_send()

    @pl.loop(1, place.planes)
    def _(k):
        plane_copy(k).wait_send()

    @pl.loop(1, place.rings)
    def _(k):
        ring_copy(k).wait_send()


def sum_and_return(part, back, cot, lats, lons):
    tokens, features = cot.shape
    half = tokens // 2
    cols = half // SHIFT_ROWS
    planes, rings = Y * X, Z_HI * lons
    columns = part.shape[-1]
    place_sel = np.zeros((half, 32), np.float32)
    for r in range(SHIFT_ROWS):
        for c in range(SHIFT_COLS):
            place_sel[r * cols + cols - SHIFT_COLS + c, r * SHIFT_COLS + c] = 1
    return pl.pallas_call(
        functools.partial(sum_kernel, lats, lons),
        out_shape=(
            jax.ShapeDtypeStruct((tokens, features), BF16),
            jax.ShapeDtypeStruct((8, columns // lons), F32),
        ),
        in_specs=[pl.BlockSpec(memory_space=VMEM)] * 4,
        out_specs=[pl.BlockSpec(memory_space=VMEM)] * 2,
        scratch_shapes=[
            VMEM((planes, 16, columns), BF16),
            VMEM((planes, 16, columns), BF16),
            VMEM((planes, 16, columns), BF16),
            VMEM((16, columns), F32),
            VMEM((rings, 16, 128), BF16),
            VMEM((rings, 16, 128), BF16),
            VMEM((half, features), BF16),
            VMEM((2, 32, features), BF16),
            pltpu.SemaphoreType.DMA((planes,)),
            pltpu.SemaphoreType.DMA((planes,)),
            pltpu.SemaphoreType.DMA((planes,)),
            pltpu.SemaphoreType.DMA((planes,)),
            pltpu.SemaphoreType.DMA((rings,)),
            pltpu.SemaphoreType.DMA((rings,)),
            pltpu.SemaphoreType.DMA((3,)),
            pltpu.SemaphoreType.DMA((3,)),
        ],
        compiler_params=pltpu.CompilerParams(
            collective_id=1, has_side_effects=True, vmem_limit_bytes=32 * 2**20
        ),
        name="sum_and_return",
    )(part, back, cot, jnp.asarray(place_sel, BF16))


PAD = 80
GROUP = 8


def contract(left, right, dims):
    return lax.dot_general(left, right, (dims, ((), ())), preferred_element_type=F32)


def compute_kernel(
    counts, tok, cot, row_tok, row_cot, side, w, take_own, take_row, take_side, row_of, head_mask,
    give, part, back, hidden, normed, spread, out_grad, qkv, qkv_grad,
):
    windows = tok.shape[0] // (WIN_ROWS * WIN_COLS)
    features = tok.shape[1]
    width = GROUP * HEAD_DIM
    lat = lax.axis_index("lat")
    own_count = counts[lat]
    previous = jnp.where(lat > 0, counts[jnp.maximum(lat - 1, 0)], 0)
    rows = row_of[...]
    limit = jnp.where(rows < SHIFT_ROWS, previous - SHIFT_ROWS, own_count + SHIFT_ROWS)
    valid = jnp.where(rows < jnp.minimum(limit, WIN_ROWS), 1.0, 0.0)

    framed = (
        jnp.dot(take_own[...], tok[...], preferred_element_type=F32)
        + jnp.dot(take_row[...], row_tok[...], preferred_element_type=F32)
        + jnp.dot(take_side[0], side[0], preferred_element_type=F32)
        + jnp.dot(take_side[1], side[1], preferred_element_type=F32)
    )
    center = framed - jnp.mean(framed, axis=-1, keepdims=True)
    inverse = lax.rsqrt(jnp.mean(center * center, axis=-1, keepdims=True) + EPSILON)
    normal = center * inverse
    normed[...] = normal
    spread[...] = jnp.broadcast_to(inverse, spread.shape)
    hidden[...] = normal.astype(BF16)
    framed = (
        jnp.dot(take_own[...], cot[...], preferred_element_type=F32)
        + jnp.dot(take_row[...], row_cot[...], preferred_element_type=F32)
        + jnp.dot(take_side[2], side[0], preferred_element_type=F32)
        + jnp.dot(take_side[3], side[1], preferred_element_type=F32)
    )
    for j in range(features // 128):
        lanes = slice(j * 128, j * 128 + 128)
        out_grad[:, lanes] = jnp.where(valid > 0.0, framed[:, lanes], 0.0).astype(BF16)

    for j in range(3):
        lanes = slice(j * features, (j + 1) * features)
        qkv[:, lanes] = jnp.dot(hidden[...], w[:, lanes], preferred_element_type=F32).astype(BF16)

    factor = HEAD_DIM ** (-0.5)
    allowed = jnp.concatenate([valid[0:PAD]] * (GROUP * PAD // 128), axis=1) > 0.0
    mask = head_mask[...]

    for window in range(windows):
        at = slice(window * PAD, window * PAD + PAD)
        for group in range(features // width):
            lanes = [slice(j * features + group * width, j * features + (group + 1) * width) for j in range(3)]
            query, keyed, valued = (qkv[at, lane] for lane in lanes)
            grad = out_grad[at, lanes[0]]
            query = jnp.concatenate([query] * GROUP, axis=0) * mask
            grad = jnp.concatenate([grad] * GROUP, axis=0) * mask
            scores = contract(keyed, query, ((1,), (1,))) * factor
            scores = jnp.where(allowed, scores, -1000000000.0)
            exponent = jnp.exp(scores - jnp.max(scores, axis=0, keepdims=True))
            probs = exponent * (1.0 / jnp.sum(exponent, axis=0, keepdims=True))
            weight = contract(valued, grad, ((1,), (1,)))
            mixed = jnp.sum(probs * weight, axis=0, keepdims=True)
            score_grad = (probs * (weight - mixed) * factor).astype(BF16)
            value_grad = jnp.dot(probs.astype(BF16), grad, preferred_element_type=F32)
            key_grad = jnp.dot(score_grad, query, preferred_element_type=F32)
            turned = contract(score_grad, keyed, ((0,), (0,)))
            query_grad = turned[0:PAD] * mask[0:PAD].astype(F32)
            for h in range(1, GROUP):
                rows_h = slice(h * PAD, h * PAD + PAD)
                query_grad = query_grad + turned[rows_h] * mask[rows_h].astype(F32)
            for lane, value in zip(lanes, (query_grad, key_grad, value_grad)):
                qkv_grad[at, lane] = value.astype(BF16)

    turned_hidden = hidden[...].T
    planes = part.shape[1]
    for j in range(3 * features // width):
        lanes = slice(j * width, (j + 1) * width)
        piece = jnp.dot(turned_hidden, qkv_grad[:, lanes], preferred_element_type=F32)
        for core in range(CORES):
            for p in range(planes):
                first = (p * CORES + core) * 8
                both = [piece[z * planes * CORES * 8 + first :][0:8] for z in range(Z_HI)]
                part[core, p, :, lanes] = jnp.concatenate(both, axis=0).astype(BF16)

    hidden_grad = contract(qkv_grad[...], w[...], ((1,), (1,)))
    normal = normed[...]
    mean_grad = jnp.mean(hidden_grad, axis=-1, keepdims=True)
    mean_mixed = jnp.mean(hidden_grad * normal, axis=-1, keepdims=True)
    frame_grad = spread[...] * (hidden_grad - mean_grad - normal * mean_mixed)
    back[...] = jnp.dot(give[...], frame_grad.astype(BF16), preferred_element_type=F32).astype(BF16)


def frame_tables(cols):
    windows = cols // WIN_COLS
    total = windows * PAD
    half = SHIFT_ROWS * cols
    own = np.zeros((total, 2 * half), np.float32)
    row = np.zeros((total, half), np.float32)
    side = np.zeros((4, total, 48), np.float32)
    give = np.zeros((2 * half + 64, total), np.float32)
    row_of = np.full((total, 128), WIN_ROWS, np.int32)
    for window in range(windows):
        for r in range(WIN_ROWS):
            for c in range(WIN_COLS):
                t = window * PAD + r * WIN_COLS + c
                row_of[t] = r
                rr, g = r - SHIFT_ROWS, window * WIN_COLS + c - SHIFT_COLS
                upper = rr < 0
                if g >= 0:
                    if upper:
                        row[t, r * cols + g] = 1
                        give[half + r * cols + g, t] = 1
                    else:
                        own[t, rr * cols + g] = 1
                        give[rr * cols + g, t] = 1
                else:
                    at = (r % SHIFT_ROWS) * SHIFT_COLS + g + SHIFT_COLS
                    side[int(upper), t, at] = 1
                    side[2 + int(upper), t, 18 + at] = 1
                    give[2 * half + 32 * int(upper) + at, t] = 1
    return own, row, side, give, row_of


def compute(counts, tok, cot, row_tok, row_cot, side, w):
    tokens, features = tok.shape
    cols = tokens // (2 * SHIFT_ROWS)
    take_own, take_row, take_side, give, row_of = frame_tables(cols)
    total = take_own.shape[0]
    width = GROUP * HEAD_DIM
    head_mask = np.zeros((GROUP, PAD, GROUP, HEAD_DIM), np.float32)
    for h in range(GROUP):
        head_mask[h, :, h] = 1
    operands = (
        tok, cot, row_tok, row_cot, side, w,
        jnp.asarray(take_own, BF16), jnp.asarray(take_row, BF16), jnp.asarray(take_side, BF16),
        jnp.asarray(row_of), jnp.asarray(head_mask.reshape(GROUP * PAD, width), BF16),
        jnp.asarray(give, BF16),
    )
    columns = w.shape[1]
    planes = w.shape[0] // (8 * CORES * Z_HI)
    return pl.pallas_call(
        compute_kernel,
        out_shape=(
            jax.ShapeDtypeStruct((CORES, planes, 8 * Z_HI, columns), BF16),
            jax.ShapeDtypeStruct((give.shape[0], features), BF16),
        ),
        in_specs=[pl.BlockSpec(memory_space=pltpu.SMEM)] + [pl.BlockSpec(memory_space=VMEM)] * len(operands),
        out_specs=[pl.BlockSpec(memory_space=VMEM)] * 2,
        scratch_shapes=[
            VMEM((total, features), BF16),
            VMEM((total, features), F32),
            VMEM((total, features), F32),
            VMEM((total, features), BF16),
            VMEM((total, columns), BF16),
            VMEM((total, columns), BF16),
        ],
        compiler_params=pltpu.CompilerParams(vmem_limit_bytes=40 * 2**20),
        name="windows",
    )(counts, *operands)


def on_device(lats, lons, tokens, cotangent, qkv_weight, band_rows):
    tok = tokens.reshape(-1, tokens.shape[-1])
    cot = cotangent.reshape(-1, tokens.shape[-1])
    w, row_tok, row_cot, side = gather(tok, cot, qkv_weight, lats, lons)
    part, back = compute(band_rows, tok, cot, row_tok, row_cot, side, w)
    token_grad, weight_gradient = sum_and_return(part, back, cot, lats, lons)
    return token_grad.reshape(tokens.shape), weight_gradient


def solution(mesh):
    return jax.shard_map(
        functools.partial(on_device, mesh.shape["lat"], mesh.shape["lon"]),
        mesh=mesh,
        in_specs=(P("lat", "lon", None), P("lat", "lon", None), P("lat", "lon"), P()),
        out_specs=(P("lat", "lon", None), P("lat", "lon")),
        check_vma=False,
    )
```

time: 471 us -> 96.8 us (0.21)
  the two profiles are of different devices: /device:TPU:6 before, /device:TPU:8 now
where the time goes in v1:
time: 96.8 us; the launch traced here: 96.3 us
  Pallas kernels  82.6 us (85%)
  local copies, waits for them, and re-layouts  13 us (13%)
    pallas_call x1, Pallas kernels, gather(): pl.pallas_call(functools.partial(gather_kernel, lats, lons), out_shape=(j...  37.7 us
    pallas_call x1, Pallas kernels, sum_and_return(): pl.pallas_call(functools.partial(sum_kernel, lats, lons), out_shape=(jax....  37.4 us
    unnamed x30, local copies, waits for them, and re-layouts  13 us
    pallas_call x1, Pallas kernels, compute(): pl.pallas_call(compute_kernel, out_shape=(jax.ShapeDtypeStruct((CORES, pl...  7.56 us

profile of v1, /device:TPU:8, one launch (start us, length us, event | category | flops | bytes accessed | tf_op | source)
XLA Modules:
  0.0 96.3 jit_solution(10790499018830081290)
XLA Ops:
  0.6 0.0 copy-start
  0.6 1.0 copy-done
  1.6 0.0 copy-start.2
  1.6 1.0 copy-done.2
  2.6 0.0 copy-start.10
  2.6 0.8 copy-done.10
  3.4 0.0 copy-start.12
  3.4 0.7 copy-done.12
  4.0 37.7 %gather.1 = (bf16[512,1536]{1,0:T(8,128)(2,1)S(1)}, bf16[144,512]{1,0:T(8,128)(2,1)S(1)}, bf16[144,512]{1,0:T(8,128)(2,1)S(1)}, bf16[2,48,512]{2,1,0:T(8,128)(2,1)S(1)}) custom-call(bf16[288,512]{1,0:T(8,128)(2,1)S(1)} %bitcast.6, bf16[288,512]{1,0:T(8,128)(2,1)S(1)} %bitcast.3, bf16[8,192]{1,0:T(8,128)(2,1)S(1)} %copy-done.12, ...), custom_call_target="tpu_custom_call" | custom-call | tf_op jit(solution)/shard_map/gather/pallas_call | solution.py:264
  41.7 0.0 copy-start.1
  41.7 1.0 copy-done.1
  42.7 0.0 copy-start.3
  42.7 1.0 copy-done.3
  43.7 0.0 copy-start.4
  43.7 1.0 %copy-done.4 = bf16[640,256]{1,0:T(8,128)(2,1)S(1)} copy-done((bf16[640,256]{1,0:T(8,128)(2,1)S(1)}, bf16[640,256]{1,0:T(8,128)(2,1)}, u32[]{:S(2)}) %copy-start.4) | copy-done | bytes 327704
  44.6 0.0 copy-start.5
  44.6 1.0 %copy-done.5 = bf16[4,320,48]{2,1,0:T(8,128)(2,1)S(1)} copy-done((bf16[4,320,48]{2,1,0:T(8,128)(2,1)S(1)}, bf16[4,320,48]{2,1,0:T(8,128)(2,1)}, u32[]{:S(2)}) %copy-start.5) | copy-done | bytes 122904
  45.6 0.0 copy-start.6
  45.6 1.0 copy-done.6
  46.6 0.0 copy-start.7
  46.6 0.9 copy-done.7
  47.5 0.0 copy-start.8
  47.5 0.9 copy-done.8
  48.4 0.0 copy-start.9
  48.4 0.9 copy-done.9
  49.3 0.0 copy-start.13
  49.3 0.7 copy-done.13
  50.0 7.6 %windows.1 = (bf16[2,16,16,1536]{3,2,1,0:T(8,128)(2,1)S(1)}, bf16[352,512]{1,0:T(8,128)(2,1)S(1)}) custom-call(s32[64]{0:T(128)S(1)} %copy-done.13, bf16[288,512]{1,0:T(8,128)(2,1)S(1)} %bitcast.7, bf16[288,512]{1,0:T(8,128)(2,1)S(1)} %bitcast.4, bf16[144,512]{1,0:T(8,128)(2,1)S(1)} %get-tuple-element.10.row_tok, ...), custom_call_target="tpu_custom_call" | custom-call | tf_op jit(solution)/shard_map/windows/pallas_call | solution.py:625
  57.6 0.0 copy-done.11
  57.6 37.4 %sum_and_return.1 = (bf16[288,512]{1,0:T(8,128)(2,1)S(1)}, f32[8,192]{1,0:T(8,128)S(1)}) custom-call(bf16[2,16,16,1536]{3,2,1,0:T(8,128)(2,1)S(1)} %get-tuple-element.14.part, bf16[352,512]{1,0:T(8,128)(2,1)S(1)} %get-tuple-element.15.back, bf16[288,512]{1,0:T(8,128)(2,1)S(1)} %bitcast.5, bf16[144,32]{1,0:T(8,128)(2,1)S(1)} %copy-done.11), custom_call_target="tpu_custom_call" | custom-call | tf_op jit(solution)/shard_map/sum_and_return/pallas_call | solution.py:448
  94.9 0.7 copy.16
  95.7 0.6 copy.17
  (1 shorter events, 0.0 us)
Async XLA Ops:
  0.6 1.0 %copy-start = (bf16[6,48,512]{2,1,0:T(8,128)(2,1)S(1)}, bf16[6,48,512]{2,1,0:T(8,128)(2,1)}, u32[]{:S(2)}) copy-start(bf16[6,48,512]{2,1,0:T(8,128)(2,1)} %param.13) | copy-start | bytes 884740
  1.6 1.0 copy-start.2
  2.6 0.8 copy-start.10
  3.4 0.7 copy-start.12
  41.7 1.0 %copy-start.1 = (bf16[6,48,512]{2,1,0:T(8,128)(2,1)S(1)}, bf16[6,48,512]{2,1,0:T(8,128)(2,1)}, u32[]{:S(2)}) copy-start(bf16[6,48,512]{2,1,0:T(8,128)(2,1)} %param.13) | copy-start | bytes 884740
  42.7 1.0 copy-start.3
  43.7 1.0 %copy-start.4 = (bf16[640,256]{1,0:T(8,128)(2,1)S(1)}, bf16[640,256]{1,0:T(8,128)(2,1)}, u32[]{:S(2)}) copy-start(bf16[640,256]{1,0:T(8,128)(2,1)} %constant.21.clone.head_mask) | copy-start | bytes 983044
  44.6 1.0 %copy-start.5 = (bf16[4,320,48]{2,1,0:T(8,128)(2,1)S(1)}, bf16[4,320,48]{2,1,0:T(8,128)(2,1)}, u32[]{:S(2)}) copy-start(bf16[4,320,48]{2,1,0:T(8,128)(2,1)} %constant.19.clone.take_side) | copy-start | bytes 368644
  45.6 1.0 copy-start.6
  46.6 0.9 copy-start.7
  47.5 0.9 copy-start.8
  48.4 0.9 copy-start.9
  49.3 0.7 copy-start.13
  50.0 7.6 %copy-start.11 = (bf16[144,32]{1,0:T(8,128)(2,1)S(1)}, bf16[144,32]{1,0:T(8,128)(2,1)}, u32[]{:S(2)}) copy-start(bf16[144,32]{1,0:T(8,128)(2,1)} %constant.23.clone.place_sel) | copy-start | bytes 27652

commit v2 on v0

v2 whole, which is shorter than its diff:
```python
import functools

import jax
import jax.numpy as jnp
import numpy as np
from jax import lax
from jax.experimental import pallas as pl
from jax.experimental.pallas import tpu as pltpu
from jax.sharding import PartitionSpec as P

MESH = pl.DeviceIdType.MESH
VMEM = pltpu.VMEM
BF16 = jnp.bfloat16
F32 = jnp.float32

WIN_ROWS = 6
WIN_COLS = 12
SHIFT_ROWS = 3
SHIFT_COLS = 6
HEAD_DIM = 32
EPSILON = 1e-05

Z_HI, Y, X, CORES = 2, 4, 4, 2


class Place:
    def __init__(self, lats, lons):
        self.lats, self.lons = lats, lons
        self.planes = Y * X
        self.rings = Z_HI * lons
        self.lat = lax.axis_index("lat")
        self.lon = lax.axis_index("lon")
        self.z_hi = self.lat // (self.planes * CORES)
        self.p = (self.lat % (self.planes * CORES)) // CORES
        self.core = self.lat % CORES
        self.z = self.z_hi * lons + self.lon

    def ring_at(self, z):
        return ((z // self.lons) * self.planes * CORES + self.p * CORES + self.core, z % self.lons)

    def plane_at(self, p):
        return (self.z_hi * self.planes * CORES + p * CORES + self.core, self.lon)

    def ring_index(self, k):
        return (self.z + k) % self.rings

    def plane_index(self, k):
        x = (self.p % X + k % X) % X
        y = (self.p // X + k // X) % Y
        return y * X + x

    def partner(self):
        return (self.lat + 1 - 2 * self.core, self.lon)

    def east(self):
        return (self.lon + 1) % self.lons

    def west(self):
        return (self.lon + self.lons - 1) % self.lons


def remote(src, dst, send, recv, device):
    return pltpu.make_async_remote_copy(
        src_ref=src, dst_ref=dst, send_sem=send, recv_sem=recv, device_id=device, device_id_type=MESH
    )


OUT_COLUMNS = ((X - 1, Y - 1), (0, Y - 1), (X - 1, 0), (0, 0), (X - 2, Y - 1), (0, 1))
BACK_COLUMNS = ((0, 0), (X - 1, 0), (0, Y - 1))
PIECE = 48

PAD = 80
GROUP = 8
HALVES = 2


class Relays:
    def __init__(self, place):
        self.last_low = place.planes * CORES - 1
        self.first_high = place.planes * CORES
        self.low_end = place.lat == self.last_low
        self.high_end = place.lat == self.first_high
        self.out = [(y * X + x) * CORES + CORES - 1 for x, y in OUT_COLUMNS]
        self.back = [self.first_high + (y * X + x) * CORES for x, y in BACK_COLUMNS]


def enter(place, relays):
    barrier = pltpu.get_barrier_semaphore()

    def signal(device):
        pl.semaphore_signal(barrier, inc=1, device_id=device, device_id_type=MESH)

    half = place.rings // 2

    @pl.loop(0, half)
    def _(k):
        signal(place.ring_at(place.ring_index(half - k)))

        @pl.when(k < half - 1)
        def _():
            signal(place.ring_at(place.ring_index(half + 1 + k)))

    @pl.loop(1, place.planes)
    def _(k):
        signal(place.plane_at(place.plane_index(k)))

    signal(place.partner())
    signal((place.lat, place.east()))
    signal((place.lat, place.west()))
    not_first = place.lat > 0
    not_last = place.lat < place.lats - 1

    @pl.when(not_first)
    def _():
        signal((place.lat - 1, place.lon))
        signal((place.lat - 1, place.west()))

    @pl.when(not_last)
    def _():
        signal((place.lat + 1, place.lon))
        signal((place.lat + 1, place.east()))

    count = place.rings + place.planes + 1
    count = count + jnp.where(not_first, 2, 0) + jnp.where(not_last, 2, 0)
    for ends, relay_of, far_end in (
        (relays.high_end, relays.out, relays.first_high),
        (relays.low_end, relays.back, relays.last_low),
    ):
        for lat in relay_of[1:]:
            @pl.when(ends)
            def _():
                signal((lat, place.lon))

            @pl.when(place.lat == lat)
            def _():
                signal((far_end, place.lon))

            count = count + jnp.where(place.lat == lat, 1, 0)
        count = count + jnp.where(ends, len(relay_of) - 1, 0)
    pl.semaphore_wait(barrier, count)


def contract(left, right, dims):
    return lax.dot_general(left, right, (dims, ((), ())), preferred_element_type=F32)


def kernel(
    lats, lons, names, *refs
):
    r = dict(zip(names, refs))
    place = Place(lats, lons)
    relays = Relays(place)
    tok, cot = r["tok"], r["cot"]
    half_rows = tok.shape[0] // 2
    features = tok.shape[1]
    width = GROUP * HEAD_DIM
    planes, rings = place.planes, place.rings
    lane_of = lax.broadcasted_iota(jnp.int32, (8, 128), 1)
    not_first = place.lat > 0
    not_last = place.lat < lats - 1
    either_end = jnp.logical_or(relays.low_end, relays.high_end)

    loads = [
        pltpu.make_async_copy(r["hbm_" + name], r[name], r["load_sem"].at[i])
        for i, name in enumerate(LOADED)
    ]
    for load in loads:
        load.start()

    wide, unit, units = r["wide"], r["unit"], r["units"]
    wide[...] = jnp.zeros_like(wide)
    wide[:, 0 : r["w_in"].shape[1]] = r["w_in"][...].astype(F32)
    unit[...] = jnp.concatenate([wide[:, 0:128], wide[:, 128:256]], axis=0).astype(BF16)
    units[place.z] = unit[...]
    for load in loads:
        load.wait()

    packed, side, sel = r["packed"], r["side"], r["sel"]
    for part_of in range(2):
        rows = pl.ds(part_of * half_rows, half_rows)
        packed[part_of] = (
            jnp.dot(sel[0], tok[rows], preferred_element_type=F32)
            + jnp.dot(sel[1], cot[rows], preferred_element_type=F32)
        ).astype(BF16)

    @pl.when(jnp.logical_not(not_first))
    def _():
        side[1] = jnp.zeros(side.shape[1:], BF16)
        r["row_tok"][...] = jnp.zeros_like(r["row_tok"])
        r["row_cot"][...] = jnp.zeros_like(r["row_cot"])

    @pl.when(jnp.logical_not(not_last))
    def _():
        r["row_back"][...] = jnp.zeros_like(r["row_back"])
        r["side_back"][1] = jnp.zeros(r["side_back"].shape[1:], BF16)

    enter(place, relays)

    def ring_copy(k):
        return remote(
            unit, units.at[place.z], r["ring_send"].at[k], r["ring_recv"].at[place.z],
            place.ring_at(place.ring_index(k)),
        )

    def ring_arrival(k):
        z = place.ring_index(k)
        return remote(unit, units.at[z], r["ring_send"].at[k], r["ring_recv"].at[z], place.ring_at(z))

    @pl.loop(1, rings)
    def _(k):
        ring_copy(k).start()

    halo_send, halo_recv = r["halo_send"], r["halo_recv"]
    side_copy = remote(packed.at[0], side.at[0], halo_send.at[0], halo_recv.at[0], (place.lat, place.east()))
    diag_copy = remote(
        packed.at[1], side.at[1], halo_send.at[1], halo_recv.at[1], (place.lat + 1, place.east())
    )

    def out_piece(i):
        rows = pl.ds((i % 3) * PIECE, PIECE)
        source = (tok if i < 3 else cot).at[pl.ds(half_rows + (i % 3) * PIECE, PIECE)]
        return source, (r["row_tok"] if i < 3 else r["row_cot"]).at[rows]

    def back_piece(i):
        source = r["back"].at[pl.ds(half_rows + i * PIECE, PIECE)]
        return source, r["row_back"].at[pl.ds(i * PIECE, PIECE)]

    class Crossing:
        def __init__(self, piece, relay_of, end, target, far_end, send, recv, sends, receives, relay, relay_sem):
            self.count = len(relay_of)
            self.relay_of, self.end, self.sends, self.receives = relay_of, end, sends, receives
            self.direct, self.via, self.onward = [], [], []
            for i in range(self.count):
                source, landing = piece(i)
                self.direct.append(remote(source, landing, send.at[i], recv.at[i], (target, place.lon)))
                self.via.append(
                    remote(source, relay, send.at[i], relay_sem.at[0], (relay_of[i], place.lon))
                )
                self.onward.append(remote(relay, landing, relay_sem.at[1], recv.at[i], (far_end, place.lon)))

        def start(self):
            plain = jnp.logical_and(self.sends, jnp.logical_not(self.end))

            @pl.when(self.end)
            def _():
                for i in range(1, self.count):
                    self.via[i].start()
                self.direct[0].start()

            @pl.when(plain)
            def _():
                for i in range(self.count):
                    self.direct[i].start()

        def pass_on(self):
            for i in range(1, self.count):
                @pl.when(place.lat == self.relay_of[i])
                def _():
                    self.via[i].wait_recv()
                    self.onward[i].start()

        def wait_recv(self):
            @pl.when(self.receives)
            def _():
                for i in range(self.count):
                    self.direct[i].wait_recv()

        def wait_send(self):
            @pl.when(self.sends)
            def _():
                for i in range(self.count):
                    self.direct[i].wait_send()

            for i in range(1, self.count):
                @pl.when(place.lat == self.relay_of[i])
                def _():
                    self.onward[i].wait_send()

    rows_out = Crossing(
        out_piece, relays.out, relays.low_end, place.lat + 1, relays.first_high,
        r["out_send"], r["out_recv"], not_last, not_first, r["relay"], r["relay_sem"],
    )
    rows_back = Crossing(
        back_piece, relays.back, relays.high_end, place.lat - 1, relays.last_low,
        r["back_send"], r["back_recv"], not_first, not_last, r["relay_back"], r["relay_back_sem"],
    )
    rows_out.start()
    side_copy.start()

    @pl.when(not_last)
    def _():
        diag_copy.start()

    @pl.loop(1, rings)
    def _(k):
        ring_arrival(k).wait_recv()

    blocks = r["blocks"]

    def tile_at(n):
        which, within = divmod(n, features // 128)
        half, at = divmod(within, width // 128)
        return half, pl.ds(which * width + at * 128, 128)

    for pair in range(lons // 2):
        tiles = [[], [], []]
        for z_hi in range(Z_HI):
            even = units[z_hi * lons + 2 * pair].astype(F32)
            odd = units[z_hi * lons + 2 * pair + 1].astype(F32)
            turned_top = pltpu.roll(odd[0:8], 64, 1)
            turned_low = pltpu.roll(odd[8:16], 64, 1)
            tiles[0].append(even[0:8])
            tiles[1].append(jnp.where(lane_of < 64, even[8:16], turned_top))
            tiles[2].append(jnp.where(lane_of < 64, turned_top, turned_low))
        for j in range(3):
            half, lanes = tile_at(pair * 3 + j)
            blocks[half, place.core, place.p, :, lanes] = jnp.concatenate(tiles[j], axis=0).astype(BF16)

    def plane_copy(half, k):
        own = blocks.at[half, place.core, place.p]
        return remote(
            own, own, r["plane_send"].at[half, k], r["plane_recv"].at[half, place.p],
            place.plane_at(place.plane_index(k)),
        )

    def plane_arrival(half, k):
        p = place.plane_index(k)
        block = blocks.at[half, place.core, p]
        return remote(block, block, r["plane_send"].at[half, k], r["plane_recv"].at[half, p], place.plane_at(p))

    def core_copy(half, p):
        block = blocks.at[half, place.core, p]
        return remote(block, block, r["core_send"].at[half, p], r["core_recv"].at[half, p], place.partner())

    def core_arrival(half, p):
        block = blocks.at[half, 1 - place.core, p]
        return remote(block, block, r["core_send"].at[half, p], r["core_recv"].at[half, p], place.partner())

    for half in range(HALVES):
        @pl.loop(1, planes)
        def _(k):
            plane_copy(half, k).start()

        core_copy(half, place.p).start()

    rows_out.pass_on()

    rows_out.wait_recv()
    side_copy.wait_recv()

    @pl.when(not_first)
    def _():
        diag_copy.wait_recv()

    own_count = r["counts"][place.lat]
    previous = jnp.where(not_first, r["counts"][jnp.maximum(place.lat - 1, 0)], 0)
    row_of = r["row_of"][...]
    limit = jnp.where(row_of < SHIFT_ROWS, previous - SHIFT_ROWS, own_count + SHIFT_ROWS)
    valid = jnp.where(row_of < jnp.minimum(limit, WIN_ROWS), 1.0, 0.0)
    take_own, take_row, take_side = r["take_own"], r["take_row"], r["take_side"]

    def framed_of(own, row, first):
        return (
            jnp.dot(take_own[...], own[...], preferred_element_type=F32)
            + jnp.dot(take_row[...], row[...], preferred_element_type=F32)
            + jnp.dot(take_side[first], side[0], preferred_element_type=F32)
            + jnp.dot(take_side[first + 1], side[1], preferred_element_type=F32)
        )

    hidden, normed, spread, out_grad = r["hidden"], r["normed"], r["spread"], r["out_grad"]
    framed = framed_of(tok, r["row_tok"], 0)
    center = framed - jnp.mean(framed, axis=-1, keepdims=True)
    inverse = lax.rsqrt(jnp.mean(center * center, axis=-1, keepdims=True) + EPSILON)
    normal = center * inverse
    normed[...] = normal
    spread[...] = jnp.broadcast_to(inverse, spread.shape)
    hidden[...] = normal.astype(BF16)
    r["turned_hidden"][...] = normal.astype(BF16).T
    framed = framed_of(cot, r["row_cot"], 2)
    for j in range(features // 128):
        lanes = slice(j * 128, j * 128 + 128)
        out_grad[:, lanes] = jnp.where(valid > 0.0, framed[:, lanes], 0.0).astype(BF16)

    weight, qkv, qkv_grad = r["weight"], r["qkv"], r["qkv_grad"]

    def forward_arrivals(half):
        @pl.loop(1, planes)
        def _(k):
            plane_arrival(half, k).wait_recv()
            core_copy(half, place.plane_index(k)).start()

    def collect(half):
        @pl.loop(0, planes)
        def _(k):
            p = place.plane_index(k)
            core_arrival(half, p).wait_recv()
            first = blocks[half, 0, p].astype(F32)
            second = blocks[half, 1, p].astype(F32)
            for z_hi in range(Z_HI):
                take = slice(z_hi * 8, z_hi * 8 + 8)
                at = pl.multiple_of((z_hi * planes + p) * 16, 16)
                weight[half, pl.ds(at, 16), :] = jnp.concatenate([first[take], second[take]], axis=0).astype(BF16)

    factor = HEAD_DIM ** (-0.5)
    allowed = jnp.concatenate([valid[0:PAD]] * (GROUP * PAD // 128), axis=1) > 0.0
    mask = r["head_mask"][...]
    windows = hidden.shape[0] // PAD

    def project(half):
        qkv[half] = jnp.dot(hidden[...], weight[half], preferred_element_type=F32).astype(BF16)

    def attend(half):
        for window in range(windows):
            at = slice(window * PAD, window * PAD + PAD)
            lanes = [slice(j * width, (j + 1) * width) for j in range(3)]
            query, keyed, valued = (qkv[half, at, lane] for lane in lanes)
            grad = out_grad[at, half * width : (half + 1) * width]
            query = jnp.concatenate([query] * GROUP, axis=0) * mask
            grad = jnp.concatenate([grad] * GROUP, axis=0) * mask
            scores = contract(keyed, query, ((1,), (1,))) * factor
            scores = jnp.where(allowed, scores, -1000000000.0)
            exponent = jnp.exp(scores - jnp.max(scores, axis=0, keepdims=True))
            probs = exponent * (1.0 / jnp.sum(exponent, axis=0, keepdims=True))
            weight_grad = contract(valued, grad, ((1,), (1,)))
            mixed = jnp.sum(probs * weight_grad, axis=0, keepdims=True)
            score_grad = (probs * (weight_grad - mixed) * factor).astype(BF16)
            value_grad = jnp.dot(probs.astype(BF16), grad, preferred_element_type=F32)
            key_grad = jnp.dot(score_grad, query, preferred_element_type=F32)
            turned = contract(score_grad, keyed, ((0,), (0,)))
            query_grad = turned[0:PAD] * mask[0:PAD].astype(F32)
            for h in range(1, GROUP):
                rows_h = slice(h * PAD, h * PAD + PAD)
                query_grad = query_grad + turned[rows_h] * mask[rows_h].astype(F32)
            for lane, value in zip(lanes, (query_grad, key_grad, value_grad)):
                qkv_grad[half, at, lane] = value.astype(BF16)

    part = r["part"]

    def weigh(half):
        for j in range(3):
            lanes = slice(j * width, (j + 1) * width)
            piece = jnp.dot(r["turned_hidden"][...], qkv_grad[half, :, lanes], preferred_element_type=F32)
            for core in range(CORES):
                for p in range(planes):
                    first = (p * CORES + core) * 8
                    both = [piece[z * planes * CORES * 8 + first :][0:8] for z in range(Z_HI)]
                    part[half, core, p, :, lanes] = jnp.concatenate(both, axis=0).astype(BF16)

    from_core, sums, from_plane, total = r["from_core"], r["sums"], r["from_plane"], r["total"]

    def core_part(half, p):
        return remote(
            part.at[half, 1 - place.core, p], from_core.at[half, p],
            r["core_part_send"].at[half, p], r["core_part_recv"].at[half, p], place.partner(),
        )

    def plane_part(half, k):
        p = place.plane_index(k)
        return remote(
            sums.at[half, p], from_plane.at[half, place.p],
            r["plane_part_send"].at[half, p], r["plane_part_recv"].at[half, place.p], place.plane_at(p),
        )

    def plane_part_arrival(half, k):
        p = place.plane_index(k)
        return remote(
            sums.at[half, p], from_plane.at[half, p],
            r["plane_part_send"].at[half, p], r["plane_part_recv"].at[half, p], place.plane_at(p),
        )

    def send_core(half):
        @pl.loop(0, planes)
        def _(k):
            core_part(half, place.plane_index(k + 1)).start()

    def send_plane(half):
        @pl.loop(0, planes)
        def _(k):
            p = place.plane_index(k + 1)
            core_part(half, p).wait_recv()
            sums[half, p] = (part[half, place.core, p].astype(F32) + from_core[half, p].astype(F32)).astype(BF16)

            @pl.when(k < planes - 1)
            def _():
                plane_part(half, k + 1).start()

    def add_plane(half):
        total[half] = sums[half, place.p].astype(F32)

        @pl.loop(1, planes)
        def _(k):
            plane_part_arrival(half, k).wait_recv()
            total[half] += from_plane[half, place.plane_index(k)].astype(F32)

    forward_arrivals(0)
    collect(0)
    project(0)
    attend(0)
    weigh(0)
    send_core(0)
    forward_arrivals(1)
    collect(1)
    project(1)
    send_plane(0)
    attend(1)
    weigh(1)
    send_core(1)

    back, side_back = r["back"], r["side_back"]
    hidden_grad = contract(qkv_grad[0], weight[0], ((1,), (1,))) + contract(qkv_grad[1], weight[1], ((1,), (1,)))
    normal = normed[...]
    mean_grad = jnp.mean(hidden_grad, axis=-1, keepdims=True)
    mean_mixed = jnp.mean(hidden_grad * normal, axis=-1, keepdims=True)
    frame_grad = spread[...] * (hidden_grad - mean_grad - normal * mean_mixed)
    back[...] = jnp.dot(r["give"][...], frame_grad.astype(BF16), preferred_element_type=F32).astype(BF16)
    side_return = remote(
        back.at[pl.ds(2 * half_rows, 32)], side_back.at[0], halo_send.at[2], halo_recv.at[2],
        (place.lat, place.west()),
    )
    diag_return = remote(
        back.at[pl.ds(2 * half_rows + 32, 32)], side_back.at[1], halo_send.at[3], halo_recv.at[3],
        (place.lat - 1, place.west()),
    )
    rows_back.start()
    side_return.start()

    @pl.when(not_first)
    def _():
        diag_return.start()

    send_plane(1)
    rows_back.pass_on()
    add_plane(0)
    add_plane(1)

    part_units, from_ring = r["part_units"], r["from_ring"]

    def ring_part(k):
        z = place.ring_index(k)
        return remote(
            part_units.at[z], from_ring.at[place.z], r["ring_part_send"].at[z],
            r["ring_part_recv"].at[place.z], place.ring_at(z),
        )

    def ring_part_arrival(k):
        z = place.ring_index(k)
        return remote(
            part_units.at[z], from_ring.at[z], r["ring_part_send"].at[z], r["ring_part_recv"].at[z],
            place.ring_at(z),
        )

    for pair in range(lons // 2):
        for z_hi in range(Z_HI):
            tiles = []
            for j in range(3):
                half, lanes = tile_at(pair * 3 + j)
                tiles.append(total[half, pl.ds(z_hi * 8, 8), lanes])
            turned = [pltpu.roll(tile, 64, 1) for tile in tiles]
            part_units[z_hi * lons + 2 * pair] = jnp.concatenate([tiles[0], tiles[1]], axis=0).astype(BF16)
            part_units[z_hi * lons + 2 * pair + 1] = jnp.concatenate(
                [jnp.where(lane_of < 64, turned[1], turned[2]), turned[2]], axis=0
            ).astype(BF16)

    @pl.loop(1, rings)
    def _(k):
        ring_part(k).start()

    from_ring[place.z] = part_units[place.z]

    rows_back.wait_recv()
    side_return.wait_recv()

    @pl.when(not_last)
    def _():
        diag_return.wait_recv()

    for part_of in range(2):
        rows = pl.ds(part_of * half_rows, half_rows)
        inner = back[0:half_rows] if part_of == 0 else r["row_back"][...]
        outer = jnp.dot(r["place_sel"][...], side_back[part_of], preferred_element_type=F32)
        r["token_grad"][rows] = (cot[rows].astype(F32) + (inner.astype(F32) + outer)).astype(BF16)

    @pl.loop(1, rings)
    def _(k):
        ring_part_arrival(k).wait_recv()

    result = from_ring[0].astype(F32)
    for z in range(1, rings):
        result = result + from_ring[z].astype(F32)
    r["weight_gradient"][:, 0:128] = result[0:8]
    r["weight_gradient"][:, 128:192] = result[8:16, 0:64]

    rows_out.wait_send()
    rows_back.wait_send()
    side_copy.wait_send()
    side_return.wait_send()

    @pl.when(not_last)
    def _():
        diag_copy.wait_send()

    @pl.when(not_first)
    def _():
        diag_return.wait_send()

    @pl.loop(1, rings)
    def _(k):
        ring_copy(k).wait_send()
        ring_part(k).wait_send()

    for half in range(HALVES):
        @pl.loop(1, planes)
        def _(k):
            plane_copy(half, k).wait_send()
            plane_part(half, k).wait_send()

        @pl.loop(0, planes)
        def _(k):
            core_copy(half, k).wait_send()
            core_part(half, k).wait_send()


LOADED = ("tok", "cot", "sel", "row_of", "take_own", "take_row", "take_side", "head_mask", "give", "place_sel")


def frame_tables(cols):
    windows = cols // WIN_COLS
    total = windows * PAD
    half = SHIFT_ROWS * cols
    own = np.zeros((total, 2 * half), np.float32)
    row = np.zeros((total, half), np.float32)
    side = np.zeros((4, total, 48), np.float32)
    give = np.zeros((2 * half + 64, total), np.float32)
    row_of = np.full((total, 128), WIN_ROWS, np.int32)
    for window in range(windows):
        for r in range(WIN_ROWS):
            for c in range(WIN_COLS):
                t = window * PAD + r * WIN_COLS + c
                row_of[t] = r
                rr, g = r - SHIFT_ROWS, window * WIN_COLS + c - SHIFT_COLS
                upper = rr < 0
                if g >= 0:
                    if upper:
                        row[t, r * cols + g] = 1
                        give[half + r * cols + g, t] = 1
                    else:
                        own[t, rr * cols + g] = 1
                        give[rr * cols + g, t] = 1
                else:
                    at = (r % SHIFT_ROWS) * SHIFT_COLS + g + SHIFT_COLS
                    side[int(upper), t, at] = 1
                    side[2 + int(upper), t, 18 + at] = 1
                    give[2 * half + 32 * int(upper) + at, t] = 1
    return own, row, side, give, row_of


def on_device(lats, lons, tokens, cotangent, qkv_weight, band_rows):
    features = tokens.shape[-1]
    tok = tokens.reshape(-1, features)
    cot = cotangent.reshape(-1, features)
    count = tok.shape[0]
    half = count // 2
    cols = half // SHIFT_ROWS
    planes, rings = Y * X, Z_HI * lons
    columns = qkv_weight.shape[1] * lons
    width = GROUP * HEAD_DIM
    take_own, take_row, take_side, give, row_of = frame_tables(cols)
    total = take_own.shape[0]
    sel = np.zeros((2, 48, half), np.float32)
    place_sel = np.zeros((half, 32), np.float32)
    for row in range(SHIFT_ROWS):
        for col in range(SHIFT_COLS):
            at, edge = row * SHIFT_COLS + col, row * cols + cols - SHIFT_COLS + col
            sel[0, at, edge] = 1
            sel[1, 18 + at, edge] = 1
            place_sel[edge, at] = 1
    head_mask = np.zeros((GROUP, PAD, GROUP, HEAD_DIM), np.float32)
    for h in range(GROUP):
        head_mask[h, :, h] = 1
    low = lambda table: jnp.asarray(table, BF16)
    loaded = {
        "tok": tok, "cot": cot, "sel": low(sel), "row_of": jnp.asarray(row_of), "take_own": low(take_own),
        "take_row": low(take_row), "take_side": low(take_side),
        "head_mask": low(head_mask.reshape(GROUP * PAD, width)), "give": low(give), "place_sel": low(place_sel),
    }
    dma = pltpu.SemaphoreType.DMA
    scratch = {name: VMEM(loaded[name].shape, loaded[name].dtype) for name in LOADED}
    scratch.update(
        wide=VMEM((8, 256), F32),
        unit=VMEM((16, 128), BF16),
        units=VMEM((rings, 16, 128), BF16),
        blocks=VMEM((HALVES, CORES, planes, 16, columns // HALVES), BF16),
        packed=VMEM((2, 48, features), BF16),
        side=VMEM((2, 48, features), BF16),
        row_tok=VMEM((half, features), BF16),
        row_cot=VMEM((half, features), BF16),
        relay=VMEM((PIECE, features), BF16),
        relay_back=VMEM((PIECE, features), BF16),
        weight=VMEM((HALVES, features, columns // HALVES), BF16),
        hidden=VMEM((total, features), BF16),
        turned_hidden=VMEM((features, total), BF16),
        normed=VMEM((total, features), F32),
        spread=VMEM((total, features), F32),
        out_grad=VMEM((total, features), BF16),
        qkv=VMEM((HALVES, total, columns // HALVES), BF16),
        qkv_grad=VMEM((HALVES, total, columns // HALVES), BF16),
        part=VMEM((HALVES, CORES, planes, 16, columns // HALVES), BF16),
        from_core=VMEM((HALVES, planes, 16, columns // HALVES), BF16),
        sums=VMEM((HALVES, planes, 16, columns // HALVES), BF16),
        from_plane=VMEM((HALVES, planes, 16, columns // HALVES), BF16),
        total=VMEM((HALVES, 16, columns // HALVES), F32),
        back=VMEM(give.shape[:1] + (features,), BF16),
        row_back=VMEM((half, features), BF16),
        side_back=VMEM((2, 32, features), BF16),
        part_units=VMEM((rings, 16, 128), BF16),
        from_ring=VMEM((rings, 16, 128), BF16),
        load_sem=dma((len(LOADED),)),
        relay_sem=dma((2,)),
        relay_back_sem=dma((2,)),
    )
    for name, shape in (
        ("ring", (rings,)), ("plane", (HALVES, planes)), ("core", (HALVES, planes)), ("halo", (4,)),
        ("out", (len(OUT_COLUMNS),)), ("back", (len(BACK_COLUMNS),)), ("core_part", (HALVES, planes)),
        ("plane_part", (HALVES, planes)), ("ring_part", (rings,)),
    ):
        scratch[name + "_send"] = dma(shape)
        scratch[name + "_recv"] = dma(shape)
    names = ["counts", "w_in"] + ["hbm_" + name for name in LOADED] + ["token_grad", "weight_gradient"]
    token_grad, weight_gradient = pl.pallas_call(
        functools.partial(kernel, lats, lons, names + list(scratch)),
        out_shape=(
            jax.ShapeDtypeStruct(tok.shape, BF16),
            jax.ShapeDtypeStruct(qkv_weight.shape, F32),
        ),
        in_specs=[pl.BlockSpec(memory_space=pltpu.SMEM), pl.BlockSpec(memory_space=VMEM)]
        + [pl.BlockSpec(memory_space=pl.ANY)] * len(LOADED),
        out_specs=[pl.BlockSpec(memory_space=VMEM)] * 2,
        scratch_shapes=list(scratch.values()),
        compiler_params=pltpu.CompilerParams(
            collective_id=0, has_side_effects=True, vmem_limit_bytes=56 * 2**20
        ),
        name="sub_block",
    )(band_rows, qkv_weight, *(loaded[name] for name in LOADED))
    return token_grad.reshape(tokens.shape), weight_gradient


def solution(mesh):
    return jax.shard_map(
        functools.partial(on_device, mesh.shape["lat"], mesh.shape["lon"]),
        mesh=mesh,
        in_specs=(P("lat", "lon", None), P("lat", "lon", None), P("lat", "lon"), P()),
        out_specs=(P("lat", "lon", None), P("lat", "lon")),
        check_vma=False,
    )
```

time: 471 us -> 72.8 us (0.15)
  waiting for transfers between devices: 340 us -> 0 us
  Pallas kernels: 0 us -> 69.7 us
  blocking collectives: 48.9 us -> 0 us
  local copies, waits for them, and re-layouts: 29.4 us -> 2.3 us
  matrix products: 23.2 us -> 0 us
  between operations: 14.8 us -> 0.65 us
  starting transfers between devices: 10.1 us -> 0 us
    reduce_scatter x1 -> x0, waiting for transfers between devices: 186 us -> none  [on_device(): lax.psum_scatter(jnp.dot(hidden.T, qkv_grad, preferred_element_type=jnp.f...]
    all_gather x1 -> x0, waiting for transfers between devices: 81.4 us -> none  [on_device(): whole_weight = lax.all_gather(columns, 'lat', axis=0, tiled=True)]
    pallas_call x0 -> x1, Pallas kernels: none -> 69.7 us  [on_device(): pl.pallas_call(functools.partial(kernel, lats, lons, names + list(scratch...]
    unnamed x4 -> x0, waiting for transfers between devices: 55.7 us -> none
    all_gather x1 -> x0, blocking collectives: 48.9 us -> none  [on_device(): columns = lax.all_gather(qkv_weight, 'lon', axis=1, tiled=True)]
    dot_general x7 -> x0, matrix products: 19.3 us -> none  [the longest x4 12.7 us: product(): return jnp.einsum(form, left, right, preferred_element_type=jnp.float32)]
    ppermute x4 -> x0, waiting for transfers between devices: 17 us -> none  [the longest x2 12.1 us: from_behind(): return lax.ppermute(block, axis, route)]
    ppermute x4 -> x0, starting transfers between devices: 9.98 us -> none  [the longest x2 6.13 us: from_behind(): return lax.ppermute(block, axis, route)]
  transfers between devices with their start and end apart: 7 -> 0, of which waited for: 6 -> 0; matrix products, arithmetic and copies ran while one was open for 2% -> 0% of each run, Pallas kernels for 0% -> 0%
where the time goes in v2:
time: 72.8 us; the launch traced here: 72.6 us
  Pallas kernels  69.7 us (96%)
  local copies, waits for them, and re-layouts  2.3 us (3%)
    pallas_call x1, Pallas kernels, on_device(): pl.pallas_call(functools.partial(kernel, lats, lons, names + list(scratch...  69.7 us
    unnamed x4, local copies, waits for them, and re-layouts  2.3 us

profile of v2, /device:TPU:6, one launch (start us, length us, event | category | flops | bytes accessed | tf_op | source)
XLA Modules:
  0.0 72.6 jit_solution(8038652863179573877)
XLA Ops:
  0.6 69.7 %sub_block.1 = (bf16[288,512]{1,0:T(8,128)(2,1)}, f32[8,192]{1,0:T(8,128)}) custom-call(s32[64]{0:T(128)} %refs_0_.1, bf16[8,192]{1,0:T(8,128)(2,1)} %refs_1_.1, bf16[288,512]{1,0:T(8,128)(2,1)} %bitcast.3, bf16[288,512]{1,0:T(8,128)(2,1)} %bitcast.4, bf16[2,48,144]{2,1,0:T(8,128)(2,1)} %constant.16.clone.refs_4_, s32[320,128]{1,0:T(8,128)} %constant.17.clone.refs_5_, ...), custom_call_target="tpu_custom_call" | custom-call | tf_op jit(solution)/shard_map/sub_block/pallas_call | solution.py:729
  70.3 0.0 copy-start
  70.3 1.7 %copy.16 = bf16[6,48,512]{2,1,0:T(8,128)(2,1)} copy(bf16[6,48,512]{2,1,0:T(8,128)(2,1)} %bitcast.5) | data formatting | bytes 589824
  72.0 0.0 copy-done
  72.0 0.6 copy.17
Async XLA Ops:
  70.3 1.7 %copy-start = (f32[8,192]{1,0:T(8,128)S(1)}, f32[8,192]{1,0:T(8,128)}, u32[]{:S(2)}) copy-start(f32[8,192]{1,0:T(8,128)} %get-tuple-element.9) | copy-start | bytes 18436

commit v3 on v2

--- a/solution.py
+++ b/solution.py
@@ -1,4 +1,5 @@
 import functools
+import types
 
 import jax
 import jax.numpy as jnp
@@ -30,33 +31,33 @@
         self.rings = Z_HI * lons
         self.lat = lax.axis_index("lat")
         self.lon = lax.axis_index("lon")
-        self.z_hi = self.lat // (self.planes * CORES)
-        self.p = (self.lat % (self.planes * CORES)) // CORES
-        self.core = self.lat % CORES
+        self.z_hi = lax.div(self.lat, self.planes * CORES)
+        self.p = lax.div(lax.rem(self.lat, self.planes * CORES), CORES)
+        self.core = lax.rem(self.lat, CORES)
         self.z = self.z_hi * lons + self.lon
 
     def ring_at(self, z):
-        return ((z // self.lons) * self.planes * CORES + self.p * CORES + self.core, z % self.lons)
+        return (lax.div(z, self.lons) * self.planes * CORES + self.p * CORES + self.core, lax.rem(z, self.lons))
 
     def plane_at(self, p):
         return (self.z_hi * self.planes * CORES + p * CORES + self.core, self.lon)
 
     def ring_index(self, k):
-        return (self.z + k) % self.rings
+        return lax.rem(self.z + k, self.rings)
 
     def plane_index(self, k):
-        x = (self.p % X + k % X) % X
-        y = (self.p // X + k // X) % Y
+        x = lax.rem(lax.rem(self.p, X) + lax.rem(k, X), X)
+        y = lax.rem(lax.div(self.p, X) + lax.div(k, X), Y)
         return y * X + x
 
     def partner(self):
         return (self.lat + 1 - 2 * self.core, self.lon)
 
     def east(self):
-        return (self.lon + 1) % self.lons
+        return lax.rem(self.lon + 1, self.lons)
 
     def west(self):
-        return (self.lon + self.lons - 1) % self.lons
+        return lax.rem(self.lon + self.lons - 1, self.lons)
 
 
 def remote(src, dst, send, recv, device):
@@ -84,21 +85,20 @@
         self.back = [self.first_high + (y * X + x) * CORES for x, y in BACK_COLUMNS]
 
 
-def enter(place, relays):
+def far_first(k, count):
+    half = count // 2
+    return half + (1 - 2 * lax.rem(k, 2)) * lax.div(k + 1, 2)
+
+
+def announce(place, relays):
     barrier = pltpu.get_barrier_semaphore()
 
     def signal(device):
         pl.semaphore_signal(barrier, inc=1, device_id=device, device_id_type=MESH)
 
-    half = place.rings // 2
-
-    @pl.loop(0, half)
+    @pl.loop(0, place.rings - 1)
     def _(k):
-        signal(place.ring_at(place.ring_index(half - k)))
-
-        @pl.when(k < half - 1)
-        def _():
-            signal(place.ring_at(place.ring_index(half + 1 + k)))
+        signal(place.ring_at(place.ring_index(far_first(k, place.rings))))
 
     @pl.loop(1, place.planes)
     def _(k):
@@ -137,20 +137,21 @@
 
             count = count + jnp.where(place.lat == lat, 1, 0)
         count = count + jnp.where(ends, len(relay_of) - 1, 0)
-    pl.semaphore_wait(barrier, count)
+    return count
 
 
 def contract(left, right, dims):
     return lax.dot_general(left, right, (dims, ((), ())), preferred_element_type=F32)
 
 
-def kernel(
-    lats, lons, names, *refs
-):
-    r = dict(zip(names, refs))
+def kernel(lats, lons, loaded, names, counts, w_in, *refs):
+    sources, token_grad, weight_gradient = refs[:loaded], refs[loaded], refs[loaded + 1]
+    refs = refs[loaded + 2 :]
+    targets = refs[:loaded]
+    r = types.SimpleNamespace(**dict(zip(names, refs)))
     place = Place(lats, lons)
     relays = Relays(place)
-    tok, cot = r["tok"], r["cot"]
+    tok, cot = r.tok, r.cot
     half_rows = tok.shape[0] // 2
     features = tok.shape[1]
     width = GROUP * HEAD_DIM
@@ -161,21 +162,23 @@
     either_end = jnp.logical_or(relays.low_end, relays.high_end)
 
     loads = [
-        pltpu.make_async_copy(r["hbm_" + name], r[name], r["load_sem"].at[i])
-        for i, name in enumerate(LOADED)
+        pltpu.make_async_copy(source, target, r.load_sem.at[i])
+        for i, (source, target) in enumerate(zip(sources, targets))
     ]
     for load in loads:
         load.start()
 
-    wide, unit, units = r["wide"], r["unit"], r["units"]
+    expected = announce(place, relays)
+
+    wide, unit, units = r.wide, r.unit, r.units
     wide[...] = jnp.zeros_like(wide)
-    wide[:, 0 : r["w_in"].shape[1]] = r["w_in"][...].astype(F32)
+    wide[:, 0 : w_in.shape[1]] = w_in[...].astype(F32)
     unit[...] = jnp.concatenate([wide[:, 0:128], wide[:, 128:256]], axis=0).astype(BF16)
     units[place.z] = unit[...]
     for load in loads:
         load.wait()
 
-    packed, side, sel = r["packed"], r["side"], r["sel"]
+    packed, side, sel = r.packed, r.side, r.sel
     for part_of in range(2):
         rows = pl.ds(part_of * half_rows, half_rows)
         packed[part_of] = (
@@ -186,31 +189,32 @@
     @pl.when(jnp.logical_not(not_first))
     def _():
         side[1] = jnp.zeros(side.shape[1:], BF16)
-        r["row_tok"][...] = jnp.zeros_like(r["row_tok"])
-        r["row_cot"][...] = jnp.zeros_like(r["row_cot"])
+        r.row_tok[...] = jnp.zeros_like(r.row_tok)
+        r.row_cot[...] = jnp.zeros_like(r.row_cot)
 
     @pl.when(jnp.logical_not(not_last))
     def _():
-        r["row_back"][...] = jnp.zeros_like(r["row_back"])
-        r["side_back"][1] = jnp.zeros(r["side_back"].shape[1:], BF16)
-
-    enter(place, relays)
+        r.row_back[...] = jnp.zeros_like(r.row_back)
+        r.side_back[1] = jnp.zeros(r.side_back.shape[1:], BF16)
+
+    pl.semaphore_wait(pltpu.get_barrier_semaphore(), expected)
 
     def ring_copy(k):
         return remote(
-            unit, units.at[place.z], r["ring_send"].at[k], r["ring_recv"].at[place.z],
+            unit, units.at[place.z], r.ring_send.at[k], r.ring_recv.at[place.z],
             place.ring_at(place.ring_index(k)),
         )
 
     def ring_arrival(k):
         z = place.ring_index(k)
-        return remote(unit, units.at[z], r["ring_send"].at[k], r["ring_recv"].at[z], place.ring_at(z))
-
-    @pl.loop(1, rings)
-    def _(k):
-        ring_copy(k).start()
-
-    halo_send, halo_recv = r["halo_send"], r["halo_recv"]
+        return remote(unit, units.at[z], r.ring_send.at[k], r.ring_recv.at[z], place.ring_at(z))
+
+    def send_ring():
+        @pl.loop(0, rings - 1)
+        def _(k):
+            ring_copy(far_first(k, rings)).start()
+
+    halo_send, halo_recv = r.halo_send, r.halo_recv
     side_copy = remote(packed.at[0], side.at[0], halo_send.at[0], halo_recv.at[0], (place.lat, place.east()))
     diag_copy = remote(
         packed.at[1], side.at[1], halo_send.at[1], halo_recv.at[1], (place.lat + 1, place.east())
@@ -219,11 +223,11 @@
     def out_piece(i):
         rows = pl.ds((i % 3) * PIECE, PIECE)
         source = (tok if i < 3 else cot).at[pl.ds(half_rows + (i % 3) * PIECE, PIECE)]
-        return source, (r["row_tok"] if i < 3 else r["row_cot"]).at[rows]
+        return source, (r.row_tok if i < 3 else r.row_cot).at[rows]
 
     def back_piece(i):
-        source = r["back"].at[pl.ds(half_rows + i * PIECE, PIECE)]
-        return source, r["row_back"].at[pl.ds(i * PIECE, PIECE)]
+        source = r.back.at[pl.ds(half_rows + i * PIECE, PIECE)]
+        return source, r.row_back.at[pl.ds(i * PIECE, PIECE)]
 
     class Crossing:
         def __init__(self, piece, relay_of, end, target, far_end, send, recv, sends, receives, relay, relay_sem):
@@ -278,86 +282,79 @@
 
     rows_out = Crossing(
         out_piece, relays.out, relays.low_end, place.lat + 1, relays.first_high,
-        r["out_send"], r["out_recv"], not_last, not_first, r["relay"], r["relay_sem"],
+        r.out_send, r.out_recv, not_last, not_first, r.relay, r.relay_sem,
     )
     rows_back = Crossing(
         back_piece, relays.back, relays.high_end, place.lat - 1, relays.last_low,
-        r["back_send"], r["back_recv"], not_first, not_last, r["relay_back"], r["relay_back_sem"],
-    )
-    rows_out.start()
-    side_copy.start()
-
-    @pl.when(not_last)
-    def _():
-        diag_copy.start()
-
-    @pl.loop(1, rings)
-    def _(k):
-        ring_arrival(k).wait_recv()
-
-    blocks = r["blocks"]
+        r.back_send, r.back_recv, not_first, not_last, r.relay_back, r.relay_back_sem,
+    )
+    def send_halos():
+        rows_out.start()
+        side_copy.start()
+
+        @pl.when(not_last)
+        def _():
+            diag_copy.start()
+
+    blocks = r.blocks
 
     def tile_at(n):
         which, within = divmod(n, features // 128)
         half, at = divmod(within, width // 128)
         return half, pl.ds(which * width + at * 128, 128)
 
-    for pair in range(lons // 2):
-        tiles = [[], [], []]
-        for z_hi in range(Z_HI):
-            even = units[z_hi * lons + 2 * pair].astype(F32)
-            odd = units[z_hi * lons + 2 * pair + 1].astype(F32)
-            turned_top = pltpu.roll(odd[0:8], 64, 1)
-            turned_low = pltpu.roll(odd[8:16], 64, 1)
-            tiles[0].append(even[0:8])
-            tiles[1].append(jnp.where(lane_of < 64, even[8:16], turned_top))
-            tiles[2].append(jnp.where(lane_of < 64, turned_top, turned_low))
-        for j in range(3):
-            half, lanes = tile_at(pair * 3 + j)
-            blocks[half, place.core, place.p, :, lanes] = jnp.concatenate(tiles[j], axis=0).astype(BF16)
+    def join_ring():
+        @pl.loop(1, rings)
+        def _(k):
+            ring_arrival(k).wait_recv()
+
+        for pair in range(lons // 2):
+            tiles = [[], [], []]
+            for z_hi in range(Z_HI):
+                even = units[z_hi * lons + 2 * pair].astype(F32)
+                odd = units[z_hi * lons + 2 * pair + 1].astype(F32)
+                turned_top = pltpu.roll(odd[0:8], 64, 1)
+                turned_low = pltpu.roll(odd[8:16], 64, 1)
+                tiles[0].append(even[0:8])
+                tiles[1].append(jnp.where(lane_of < 64, even[8:16], turned_top))
+                tiles[2].append(jnp.where(lane_of < 64, turned_top, turned_low))
+            for j in range(3):
+                half, lanes = tile_at(pair * 3 + j)
+                blocks[half, place.core, place.p, :, lanes] = jnp.concatenate(tiles[j], axis=0).astype(BF16)
 
     def plane_copy(half, k):
         own = blocks.at[half, place.core, place.p]
         return remote(
-            own, own, r["plane_send"].at[half, k], r["plane_recv"].at[half, place.p],
+            own, own, r.plane_send.at[half, k], r.plane_recv.at[half, place.p],
             place.plane_at(place.plane_index(k)),
         )
 
     def plane_arrival(half, k):
         p = place.plane_index(k)
         block = blocks.at[half, place.core, p]
-        return remote(block, block, r["plane_send"].at[half, k], r["plane_recv"].at[half, p], place.plane_at(p))
+        return remote(block, block, r.plane_send.at[half, k], r.plane_recv.at[half, p], place.plane_at(p))
 
     def core_copy(half, p):
         block = blocks.at[half, place.core, p]
-        return remote(block, block, r["core_send"].at[half, p], r["core_recv"].at[half, p], place.partner())
+        return remote(block, block, r.core_send.at[half, p], r.core_recv.at[half, p], place.partner())
 
     def core_arrival(half, p):
         block = blocks.at[half, 1 - place.core, p]
-        return remote(block, block, r["core_send"].at[half, p], r["core_recv"].at[half, p], place.partner())
-
-    for half in range(HALVES):
+        return remote(block, block, r.core_send.at[half, p], r.core_recv.at[half, p], place.partner())
+
+    def send_blocks(half):
         @pl.loop(1, planes)
         def _(k):
             plane_copy(half, k).start()
 
         core_copy(half, place.p).start()
 
-    rows_out.pass_on()
-
-    rows_out.wait_recv()
-    side_copy.wait_recv()
-
-    @pl.when(not_first)
-    def _():
-        diag_copy.wait_recv()
-
-    own_count = r["counts"][place.lat]
-    previous = jnp.where(not_first, r["counts"][jnp.maximum(place.lat - 1, 0)], 0)
-    row_of = r["row_of"][...]
+    own_count = counts[place.lat]
+    previous = jnp.where(not_first, counts[jnp.maximum(place.lat - 1, 0)], 0)
+    row_of = r.row_of[...]
     limit = jnp.where(row_of < SHIFT_ROWS, previous - SHIFT_ROWS, own_count + SHIFT_ROWS)
     valid = jnp.where(row_of < jnp.minimum(limit, WIN_ROWS), 1.0, 0.0)
-    take_own, take_row, take_side = r["take_own"], r["take_row"], r["take_side"]
+    take_own, take_row, take_side = r.take_own, r.take_row, r.take_side
 
     def framed_of(own, row, first):
         return (
@@ -367,21 +364,29 @@
             + jnp.dot(take_side[first + 1], side[1], preferred_element_type=F32)
         )
 
-    hidden, normed, spread, out_grad = r["hidden"], r["normed"], r["spread"], r["out_grad"]
-    framed = framed_of(tok, r["row_tok"], 0)
-    center = framed - jnp.mean(framed, axis=-1, keepdims=True)
-    inverse = lax.rsqrt(jnp.mean(center * center, axis=-1, keepdims=True) + EPSILON)
-    normal = center * inverse
-    normed[...] = normal
-    spread[...] = jnp.broadcast_to(inverse, spread.shape)
-    hidden[...] = normal.astype(BF16)
-    r["turned_hidden"][...] = normal.astype(BF16).T
-    framed = framed_of(cot, r["row_cot"], 2)
-    for j in range(features // 128):
-        lanes = slice(j * 128, j * 128 + 128)
-        out_grad[:, lanes] = jnp.where(valid > 0.0, framed[:, lanes], 0.0).astype(BF16)
-
-    weight, qkv, qkv_grad = r["weight"], r["qkv"], r["qkv_grad"]
+    hidden, normed, spread, out_grad = r.hidden, r.normed, r.spread, r.out_grad
+    def frame():
+        rows_out.wait_recv()
+        side_copy.wait_recv()
+
+        @pl.when(not_first)
+        def _():
+            diag_copy.wait_recv()
+
+        framed = framed_of(tok, r.row_tok, 0)
+        center = framed - jnp.mean(framed, axis=-1, keepdims=True)
+        inverse = lax.rsqrt(jnp.mean(center * center, axis=-1, keepdims=True) + EPSILON)
+        normal = center * inverse
+        normed[...] = normal
+        spread[...] = jnp.broadcast_to(inverse, spread.shape)
+        hidden[...] = normal.astype(BF16)
+        r.turned_hidden[...] = normal.astype(BF16).T
+        framed = framed_of(cot, r.row_cot, 2)
+        for j in range(features // 128):
+            lanes = slice(j * 128, j * 128 + 128)
+            out_grad[:, lanes] = jnp.where(valid > 0.0, framed[:, lanes], 0.0).astype(BF16)
+
+    weight, qkv, qkv_grad = r.weight, r.qkv, r.qkv_grad
 
     def forward_arrivals(half):
         @pl.loop(1, planes)
@@ -403,7 +408,7 @@
 
     factor = HEAD_DIM ** (-0.5)
     allowed = jnp.concatenate([valid[0:PAD]] * (GROUP * PAD // 128), axis=1) > 0.0
-    mask = r["head_mask"][...]
+    mask = r.head_mask[...]
     windows = hidden.shape[0] // PAD
 
     def project(half):
@@ -434,38 +439,38 @@
             for lane, value in zip(lanes, (query_grad, key_grad, value_grad)):
                 qkv_grad[half, at, lane] = value.astype(BF16)
 
-    part = r["part"]
+    part = r.part
 
     def weigh(half):
         for j in range(3):
             lanes = slice(j * width, (j + 1) * width)
-            piece = jnp.dot(r["turned_hidden"][...], qkv_grad[half, :, lanes], preferred_element_type=F32)
+            piece = jnp.dot(r.turned_hidden[...], qkv_grad[half, :, lanes], preferred_element_type=F32)
             for core in range(CORES):
                 for p in range(planes):
                     first = (p * CORES + core) * 8
                     both = [piece[z * planes * CORES * 8 + first :][0:8] for z in range(Z_HI)]
                     part[half, core, p, :, lanes] = jnp.concatenate(both, axis=0).astype(BF16)
 
-    from_core, sums, from_plane, total = r["from_core"], r["sums"], r["from_plane"], r["total"]
+    from_core, sums, from_plane, total = r.from_core, r.sums, r.from_plane, r.total
 
     def core_part(half, p):
         return remote(
             part.at[half, 1 - place.core, p], from_core.at[half, p],
-            r["core_part_send"].at[half, p], r["core_part_recv"].at[half, p], place.partner(),
+            r.core_part_send.at[half, p], r.core_part_recv.at[half, p], place.partner(),
         )
 
     def plane_part(half, k):
         p = place.plane_index(k)
         return remote(
             sums.at[half, p], from_plane.at[half, place.p],
-            r["plane_part_send"].at[half, p], r["plane_part_recv"].at[half, place.p], place.plane_at(p),
+            r.plane_part_send.at[half, p], r.plane_part_recv.at[half, place.p], place.plane_at(p),
         )
 
     def plane_part_arrival(half, k):
         p = place.plane_index(k)
         return remote(
             sums.at[half, p], from_plane.at[half, p],
-            r["plane_part_send"].at[half, p], r["plane_part_recv"].at[half, p], place.plane_at(p),
+            r.plane_part_send.at[half, p], r.plane_part_recv.at[half, p], place.plane_at(p),
         )
 
     def send_core(half):
@@ -492,6 +497,128 @@
             plane_part_arrival(half, k).wait_recv()
             total[half] += from_plane[half, place.plane_index(k)].astype(F32)
 
+    back, side_back = r.back, r.side_back
+    side_return = remote(
+        back.at[pl.ds(2 * half_rows, 32)], side_back.at[0], halo_send.at[2], halo_recv.at[2],
+        (place.lat, place.west()),
+    )
+    diag_return = remote(
+        back.at[pl.ds(2 * half_rows + 32, 32)], side_back.at[1], halo_send.at[3], halo_recv.at[3],
+        (place.lat - 1, place.west()),
+    )
+    def differentiate():
+        hidden_grad = contract(qkv_grad[0], weight[0], ((1,), (1,))) + contract(qkv_grad[1], weight[1], ((1,), (1,)))
+        normal = normed[...]
+        mean_grad = jnp.mean(hidden_grad, axis=-1, keepdims=True)
+        mean_mixed = jnp.mean(hidden_grad * normal, axis=-1, keepdims=True)
+        frame_grad = spread[...] * (hidden_grad - mean_grad - normal * mean_mixed)
+        back[...] = jnp.dot(r.give[...], frame_grad.astype(BF16), preferred_element_type=F32).astype(BF16)
+
+    def return_halos():
+        rows_back.start()
+        side_return.start()
+
+        @pl.when(not_first)
+        def _():
+            diag_return.start()
+
+    part_units, from_ring = r.part_units, r.from_ring
+
+    def ring_part(k):
+        z = place.ring_index(k)
+        return remote(
+            part_units.at[z], from_ring.at[place.z], r.ring_part_send.at[z],
+            r.ring_part_recv.at[place.z], place.ring_at(z),
+        )
+
+    def ring_part_arrival(k):
+        z = place.ring_index(k)
+        return remote(
+            part_units.at[z], from_ring.at[z], r.ring_part_send.at[z], r.ring_part_recv.at[z],
+            place.ring_at(z),
+        )
+
+    def send_ring_parts():
+        for pair in range(lons // 2):
+            for z_hi in range(Z_HI):
+                tiles = []
+                for j in range(3):
+                    half, lanes = tile_at(pair * 3 + j)
+                    tiles.append(total[half, pl.ds(z_hi * 8, 8), lanes])
+                turned = [pltpu.roll(tile, 64, 1) for tile in tiles]
+                part_units[z_hi * lons + 2 * pair] = jnp.concatenate([tiles[0], tiles[1]], axis=0).astype(BF16)
+                part_units[z_hi * lons + 2 * pair + 1] = jnp.concatenate(
+                    [jnp.where(lane_of < 64, turned[1], turned[2]), turned[2]], axis=0
+                ).astype(BF16)
+
+        @pl.loop(0, rings - 1)
+        def _(k):
+            ring_part(far_first(k, rings)).start()
+
+        from_ring[place.z] = part_units[place.z]
+
+    def finish_tokens():
+        rows_back.wait_recv()
+        side_return.wait_recv()
+
+        @pl.when(not_last)
+        def _():
+            diag_return.wait_recv()
+
+        for part_of in range(2):
+            rows = pl.ds(part_of * half_rows, half_rows)
+            inner = back[0:half_rows] if part_of == 0 else r.row_back[...]
+            outer = jnp.dot(r.place_sel[...], side_back[part_of], preferred_element_type=F32)
+            token_grad[rows] = (cot[rows].astype(F32) + (inner.astype(F32) + outer)).astype(BF16)
+
+    def finish_weight():
+        @pl.loop(1, rings)
+        def _(k):
+            ring_part_arrival(k).wait_recv()
+
+        result = from_ring[0].astype(F32)
+        for z in range(1, rings):
+            result = result + from_ring[z].astype(F32)
+        weight_gradient[:, 0:128] = result[0:8]
+        weight_gradient[:, 128:192] = result[8:16, 0:64]
+
+    def drain():
+        rows_out.wait_send()
+        rows_back.wait_send()
+        side_copy.wait_send()
+        side_return.wait_send()
+
+        @pl.when(not_last)
+        def _():
+            diag_copy.wait_send()
+
+        @pl.when(not_first)
+        def _():
+            diag_return.wait_send()
+
+        @pl.loop(1, rings)
+        def _(k):
+            ring_copy(k).wait_send()
+            ring_part(k).wait_send()
+
+        for half in range(HALVES):
+            @pl.loop(1, planes)
+            def _(k):
+                plane_copy(half, k).wait_send()
+                plane_part(half, k).wait_send()
+
+            @pl.loop(0, planes)
+            def _(k):
+                core_copy(half, k).wait_send()
+                core_part(half, k).wait_send()
+
+    send_ring()
+    send_halos()
+    join_ring()
+    send_blocks(0)
+    send_blocks(1)
+    rows_out.pass_on()
+    frame()
     forward_arrivals(0)
     collect(0)
     project(0)
@@ -505,122 +632,16 @@
     attend(1)
     weigh(1)
     send_core(1)
-
-    back, side_back = r["back"], r["side_back"]
-    hidden_grad = contract(qkv_grad[0], weight[0], ((1,), (1,))) + contract(qkv_grad[1], weight[1], ((1,), (1,)))
-    normal = normed[...]
-    mean_grad = jnp.mean(hidden_grad, axis=-1, keepdims=True)
-    mean_mixed = jnp.mean(hidden_grad * normal, axis=-1, keepdims=True)
-    frame_grad = spread[...] * (hidden_grad - mean_grad - normal * mean_mixed)
-    back[...] = jnp.dot(r["give"][...], frame_grad.astype(BF16), preferred_element_type=F32).astype(BF16)
-    side_return = remote(
-        back.at[pl.ds(2 * half_rows, 32)], side_back.at[0], halo_send.at[2], halo_recv.at[2],
-        (place.lat, place.west()),
-    )
-    diag_return = remote(
-        back.at[pl.ds(2 * half_rows + 32, 32)], side_back.at[1], halo_send.at[3], halo_recv.at[3],
-        (place.lat - 1, place.west()),
-    )
-    rows_back.start()
-    side_return.start()
-
-    @pl.when(not_first)
-    def _():
-        diag_return.start()
-
+    differentiate()
+    return_halos()
     send_plane(1)
     rows_back.pass_on()
     add_plane(0)
     add_plane(1)
-
-    part_units, from_ring = r["part_units"], r["from_ring"]
-
-    def ring_part(k):
-        z = place.ring_index(k)
-        return remote(
-            part_units.at[z], from_ring.at[place.z], r["ring_part_send"].at[z],
-            r["ring_part_recv"].at[place.z], place.ring_at(z),
-        )
-
-    def ring_part_arrival(k):
-        z = place.ring_index(k)
-        return remote(
-            part_units.at[z], from_ring.at[z], r["ring_part_send"].at[z], r["ring_part_recv"].at[z],
-            place.ring_at(z),
-        )
-
-    for pair in range(lons // 2):
-        for z_hi in range(Z_HI):
-            tiles = []
-            for j in range(3):
-                half, lanes = tile_at(pair * 3 + j)
-                tiles.append(total[half, pl.ds(z_hi * 8, 8), lanes])
-            turned = [pltpu.roll(tile, 64, 1) for tile in tiles]
-            part_units[z_hi * lons + 2 * pair] = jnp.concatenate([tiles[0], tiles[1]], axis=0).astype(BF16)
-            part_units[z_hi * lons + 2 * pair + 1] = jnp.concatenate(
-                [jnp.where(lane_of < 64, turned[1], turned[2]), turned[2]], axis=0
-            ).astype(BF16)
-
-    @pl.loop(1, rings)
-    def _(k):
-        ring_part(k).start()
-
-    from_ring[place.z] = part_units[place.z]
-
-    rows_back.wait_recv()
-    side_return.wait_recv()
-
-    @pl.when(not_last)
-    def _():
-        diag_return.wait_recv()
-
-    for part_of in range(2):
-        rows = pl.ds(part_of * half_rows, half_rows)
-        inner = back[0:half_rows] if part_of == 0 else r["row_back"][...]
-        outer = jnp.dot(r["place_sel"][...], side_back[part_of], preferred_element_type=F32)
-        r["token_grad"][rows] = (cot[rows].astype(F32) + (inner.astype(F32) + outer)).astype(BF16)
-
-    @pl.loop(1, rings)
-    def _(k):
-        ring_part_arrival(k).wait_recv()
-
-    result = from_ring[0].astype(F32)
-    for z in range(1, rings):
-        result = result + from_ring[z].astype(F32)
-    r["weight_gradient"][:, 0:128] = result[0:8]
-    r["weight_gradient"][:, 128:192] = result[8:16, 0:64]
-
-    rows_out.wait_send()
-    rows_back.wait_send()
-    side_copy.wait_send()
-    side_return.wait_send()
-
-    @pl.when(not_last)
-    def _():
-        diag_copy.wait_send()
-
-    @pl.when(not_first)
-    def _():
-        diag_return.wait_send()
-
-    @pl.loop(1, rings)
-    def _(k):
-        ring_copy(k).wait_send()
-        ring_part(k).wait_send()
-
-    for half in range(HALVES):
-        @pl.loop(1, planes)
-        def _(k):
-            plane_copy(half, k).wait_send()
-            plane_part(half, k).wait_send()
-
-        @pl.loop(0, planes)
-        def _(k):
-            core_copy(half, k).wait_send()
-            core_part(half, k).wait_send()
-
-
-LOADED = ("tok", "cot", "sel", "row_of", "take_own", "take_row", "take_side", "head_mask", "give", "place_sel")
+    send_ring_parts()
+    finish_tokens()
+    finish_weight()
+    drain()
 
 
 def frame_tables(cols):
@@ -678,13 +699,13 @@
     for h in range(GROUP):
         head_mask[h, :, h] = 1
     low = lambda table: jnp.asarray(table, BF16)
-    loaded = {
-        "tok": tok, "cot": cot, "sel": low(sel), "row_of": jnp.asarray(row_of), "take_own": low(take_own),
-        "take_row": low(take_row), "take_side": low(take_side),
-        "head_mask": low(head_mask.reshape(GROUP * PAD, width)), "give": low(give), "place_sel": low(place_sel),
-    }
+    loaded = dict(
+        tok=tok, cot=cot, sel=low(sel), row_of=jnp.asarray(row_of), take_own=low(take_own), take_row=low(take_row),
+        take_side=low(take_side), head_mask=low(head_mask.reshape(GROUP * PAD, width)), give=low(give),
+        place_sel=low(place_sel),
+    )
     dma = pltpu.SemaphoreType.DMA
-    scratch = {name: VMEM(loaded[name].shape, loaded[name].dtype) for name in LOADED}
+    scratch = {name: VMEM(array.shape, array.dtype) for name, array in loaded.items()}
     scratch.update(
         wide=VMEM((8, 256), F32),
         unit=VMEM((16, 128), BF16),
@@ -714,33 +735,32 @@
         side_back=VMEM((2, 32, features), BF16),
         part_units=VMEM((rings, 16, 128), BF16),
         from_ring=VMEM((rings, 16, 128), BF16),
-        load_sem=dma((len(LOADED),)),
+        load_sem=dma((len(loaded),)),
         relay_sem=dma((2,)),
         relay_back_sem=dma((2,)),
     )
-    for name, shape in (
-        ("ring", (rings,)), ("plane", (HALVES, planes)), ("core", (HALVES, planes)), ("halo", (4,)),
-        ("out", (len(OUT_COLUMNS),)), ("back", (len(BACK_COLUMNS),)), ("core_part", (HALVES, planes)),
-        ("plane_part", (HALVES, planes)), ("ring_part", (rings,)),
-    ):
+    both = dict(
+        ring=(rings,), plane=(HALVES, planes), core=(HALVES, planes), halo=(4,), out=(len(OUT_COLUMNS),),
+        back=(len(BACK_COLUMNS),), core_part=(HALVES, planes), plane_part=(HALVES, planes), ring_part=(rings,),
+    )
+    for name, shape in both.items():
         scratch[name + "_send"] = dma(shape)
         scratch[name + "_recv"] = dma(shape)
-    names = ["counts", "w_in"] + ["hbm_" + name for name in LOADED] + ["token_grad", "weight_gradient"]
     token_grad, weight_gradient = pl.pallas_call(
-        functools.partial(kernel, lats, lons, names + list(scratch)),
+        functools.partial(kernel, lats, lons, len(loaded), list(scratch)),
         out_shape=(
             jax.ShapeDtypeStruct(tok.shape, BF16),
             jax.ShapeDtypeStruct(qkv_weight.shape, F32),
         ),
         in_specs=[pl.BlockSpec(memory_space=pltpu.SMEM), pl.BlockSpec(memory_space=VMEM)]
-        + [pl.BlockSpec(memory_space=pl.ANY)] * len(LOADED),
+        + [pl.BlockSpec(memory_space=pl.ANY)] * len(loaded),
         out_specs=[pl.BlockSpec(memory_space=VMEM)] * 2,
         scratch_shapes=list(scratch.values()),
         compiler_params=pltpu.CompilerParams(
             collective_id=0, has_side_effects=True, vmem_limit_bytes=56 * 2**20
         ),
         name="sub_block",
-    )(band_rows, qkv_weight, *(loaded[name] for name in LOADED))
+    )(band_rows, qkv_weight, *loaded.values())
     return token_grad.reshape(tokens.shape), weight_gradient
 
 

time: 72.8 us -> 70.3 us (0.966); the launches traced: 72.6 us -> 68.9 us
  Pallas kernels: 69.7 us -> 66 us
    pallas_call x1, Pallas kernels: 69.7 us -> 66 us  [on_device(): pl.pallas_call(functools.partial(kernel, lats, lons, len(loaded), list(sc...]
where the time goes in v3:
time: 70.3 us; the launch traced here: 68.9 us
  Pallas kernels  66 us (94%)
  local copies, waits for them, and re-layouts  2.3 us (3%)
    pallas_call x1, Pallas kernels, on_device(): pl.pallas_call(functools.partial(kernel, lats, lons, len(loaded), list(sc...  66 us
    unnamed x4, local copies, waits for them, and re-layouts  2.3 us

profile of v3, /device:TPU:6, one launch (start us, length us, event | category | flops | bytes accessed | tf_op | source)
XLA Modules:
  0.0 68.9 jit_solution(10227776800980163688)
XLA Ops:
  0.6 66.0 %sub_block.1 = (bf16[288,512]{1,0:T(8,128)(2,1)}, f32[8,192]{1,0:T(8,128)}) custom-call(s32[64]{0:T(128)} %counts.1, bf16[8,192]{1,0:T(8,128)(2,1)} %w_in.1, bf16[288,512]{1,0:T(8,128)(2,1)} %bitcast.3, bf16[288,512]{1,0:T(8,128)(2,1)} %bitcast.4, bf16[2,48,144]{2,1,0:T(8,128)(2,1)} %constant.16.clone.refs_2_, s32[320,128]{1,0:T(8,128)} %constant.17.clone.refs_3_, ...), custom_call_target="tpu_custom_call" | custom-call | tf_op jit(solution)/shard_map/sub_block/pallas_call | solution.py:749
  66.6 0.0 copy-start
  66.6 1.7 %copy.16 = bf16[6,48,512]{2,1,0:T(8,128)(2,1)} copy(bf16[6,48,512]{2,1,0:T(8,128)(2,1)} %bitcast.5) | data formatting | bytes 589824
  68.3 0.0 copy-done
  68.3 0.6 copy.17
Async XLA Ops:
  66.6 1.7 %copy-start = (f32[8,192]{1,0:T(8,128)S(1)}, f32[8,192]{1,0:T(8,128)}, u32[]{:S(2)}) copy-start(f32[8,192]{1,0:T(8,128)} %get-tuple-element.9) | copy-start | bytes 18436

commit v4 on v3

v4 whole, which is shorter than its diff:
```python
import functools
import types

import jax
import jax.numpy as jnp
import numpy as np
from jax import lax
from jax.experimental import pallas as pl
from jax.experimental.pallas import tpu as pltpu
from jax.sharding import PartitionSpec as P

MESH = pl.DeviceIdType.MESH
VMEM = pltpu.VMEM
BF16 = jnp.bfloat16
F32 = jnp.float32

WIN_ROWS = 6
WIN_COLS = 12
SHIFT_ROWS = 3
SHIFT_COLS = 6
HEAD_DIM = 32
EPSILON = 1e-05

Z_HI, Y, X, CORES = 2, 4, 4, 2


class Place:
    def __init__(self, lats, lons):
        self.lats, self.lons = lats, lons
        self.planes = Y * X
        self.rings = Z_HI * lons
        self.lat = lax.axis_index("lat")
        self.lon = lax.axis_index("lon")
        self.z_hi = lax.div(self.lat, self.planes * CORES)
        self.p = lax.div(lax.rem(self.lat, self.planes * CORES), CORES)
        self.core = lax.rem(self.lat, CORES)
        self.z = self.z_hi * lons + self.lon

    def ring_at(self, z):
        return (lax.div(z, self.lons) * self.planes * CORES + self.p * CORES + self.core, lax.rem(z, self.lons))

    def plane_at(self, p):
        return (self.z_hi * self.planes * CORES + p * CORES + self.core, self.lon)

    def ring_index(self, k):
        return lax.rem(self.z + k, self.rings)

    def plane_index(self, k):
        x = lax.rem(lax.rem(self.p, X) + lax.rem(k, X), X)
        y = lax.rem(lax.div(self.p, X) + lax.div(k, X), Y)
        return y * X + x

    def partner(self):
        return (self.lat + 1 - 2 * self.core, self.lon)

    def east(self):
        return lax.rem(self.lon + 1, self.lons)

    def west(self):
        return lax.rem(self.lon + self.lons - 1, self.lons)


def remote(src, dst, send, recv, device):
    return pltpu.make_async_remote_copy(
        src_ref=src, dst_ref=dst, send_sem=send, recv_sem=recv, device_id=device, device_id_type=MESH
    )


OUT_ROWS = (
    (0, Y - 1), (X - 1, 0), (0, 0), (1, 0), (0, 1), (X - 2, 0), (0, Y - 2), (1, Y - 1), (X - 1, 1),
)
OUT_CORNER = ((X - 2, Y - 1), (X - 1, Y - 2), (1, 1))
BACK_ROWS = (
    (X - 1, 0), (0, Y - 1), (X - 1, Y - 1), (X - 2, Y - 1), (X - 1, Y - 2), (1, Y - 1), (X - 1, 1), (X - 2, 0),
    (0, Y - 2),
)
BACK_CORNER = ((1, 0), (X - 2, Y - 2))
TILE = 16

PAD = 80
GROUP = 4


class Relays:
    def __init__(self, place):
        self.last_low = place.planes * CORES - 1
        self.first_high = place.planes * CORES
        self.low_end = place.lat == self.last_low
        self.high_end = place.lat == self.first_high

        def low(columns):
            return [(y * X + x) * CORES + CORES - 1 for x, y in columns]

        def high(columns):
            return [self.first_high + (y * X + x) * CORES for x, y in columns]

        self.out_rows, self.out_corner = low(OUT_ROWS), low(OUT_CORNER)
        self.back_rows, self.back_corner = high(BACK_ROWS), high(BACK_CORNER)


def far_first(k, count):
    half = count // 2
    return half + (1 - 2 * lax.rem(k, 2)) * lax.div(k + 1, 2)


def announce(place, relays):
    barrier = pltpu.get_barrier_semaphore()

    def signal(device):
        pl.semaphore_signal(barrier, inc=1, device_id=device, device_id_type=MESH)

    count = place.rings + place.planes - 1

    for ends, groups in (
        (relays.high_end, ((relays.out_rows, place.lon), (relays.out_corner, place.west()))),
        (relays.low_end, ((relays.back_rows, place.lon), (relays.back_corner, place.east()))),
    ):
        for lats, lon in groups:
            @pl.when(ends)
            def _():
                for lat in lats:
                    signal((lat, lon))

            for lat in lats:
                count = count + jnp.where(place.lat == lat, 1, 0)

    above = jnp.logical_and(place.lat > 0, jnp.logical_not(relays.high_end))
    below = jnp.logical_and(place.lat < place.lats - 1, jnp.logical_not(relays.low_end))

    @pl.when(above)
    def _():
        signal((place.lat - 1, place.lon))
        signal((place.lat - 1, place.west()))

    @pl.when(below)
    def _():
        signal((place.lat + 1, place.lon))
        signal((place.lat + 1, place.east()))

    count = count + jnp.where(above, 2, 0) + jnp.where(below, 2, 0)

    @pl.loop(0, place.rings - 1)
    def _(k):
        signal(place.ring_at(place.ring_index(far_first(k, place.rings))))

    @pl.loop(1, place.planes)
    def _(k):
        signal(place.plane_at(place.plane_index(k)))

    signal(place.partner())
    return count


def contract(left, right, dims):
    return lax.dot_general(left, right, (dims, ((), ())), preferred_element_type=F32)


def kernel(lats, lons, loaded, names, *refs):
    sources, returned, weight_gradient = refs[:loaded], refs[loaded], refs[loaded + 1]
    refs = refs[loaded + 2 :]
    targets = refs[:loaded]
    r = types.SimpleNamespace(**dict(zip(names, refs)))
    place = Place(lats, lons)
    relays = Relays(place)
    tok, cot = r.tok, r.cot
    half_rows = tok.shape[0] // 2
    features = tok.shape[1]
    width = GROUP * HEAD_DIM
    groups = features // width
    planes, rings = place.planes, place.rings
    lane_of = lax.broadcasted_iota(jnp.int32, (8, 128), 1)
    not_first = place.lat > 0
    not_last = place.lat < lats - 1

    loads = [
        pltpu.make_async_copy(source, target, r.load_sem.at[i])
        for i, (source, target) in enumerate(zip(sources, targets))
    ]
    for load in loads:
        load.start()

    expected = announce(place, relays)

    wide, unit, units = r.wide, r.unit, r.units
    wide[...] = jnp.zeros_like(wide)
    loads[0].wait()
    wide[:, 0 : r.w_in.shape[1]] = r.w_in[...].astype(F32)
    unit[...] = jnp.concatenate([wide[:, 0:128], wide[:, 128:256]], axis=0).astype(BF16)
    units[place.z] = unit[...]
    for load in loads[1:]:
        load.wait()

    packed, side, sel = r.packed, r.side, r.sel
    for part_of in range(2):
        rows = pl.ds(part_of * half_rows, half_rows)
        packed[part_of] = (
            jnp.dot(sel[0], tok[rows], preferred_element_type=F32)
            + jnp.dot(sel[1], cot[rows], preferred_element_type=F32)
        ).astype(BF16)

    @pl.when(jnp.logical_not(not_first))
    def _():
        side[1] = jnp.zeros(side.shape[1:], BF16)
        r.row_tok[...] = jnp.zeros_like(r.row_tok)
        r.row_cot[...] = jnp.zeros_like(r.row_cot)

    @pl.when(jnp.logical_not(not_last))
    def _():
        r.row_back[...] = jnp.zeros_like(r.row_back)
        r.side_back[1] = jnp.zeros(r.side_back.shape[1:], BF16)

    pl.semaphore_wait(pltpu.get_barrier_semaphore(), expected)

    def ring_copy(k):
        return remote(
            unit, units.at[place.z], r.ring_send.at[0], r.ring_recv.at[0], place.ring_at(place.ring_index(k))
        )

    others = pl.ds(0, rings - 1)
    ring_all = remote(units.at[others], units.at[others], r.ring_send.at[0], r.ring_recv.at[0], place.partner())

    def send_ring():
        @pl.loop(0, rings - 1)
        def _(k):
            ring_copy(far_first(k, rings)).start()

    halo_send, halo_recv = r.halo_send, r.halo_recv
    side_copy = remote(packed.at[0], side.at[0], halo_send.at[0], halo_recv.at[0], (place.lat, place.east()))

    class Crossing:
        def __init__(self, sources, landings, lats, end, sends, receives, target, far, send, recv, relay, relay_sem):
            self.lats, self.end, self.sends, self.receives = lats, end, sends, receives
            self.direct, self.via, self.onward = [], [[] for _ in lats], [[] for _ in lats]
            for j, (source, landing) in enumerate(zip(sources, landings)):
                self.direct.append(remote(source, landing, send.at[j], recv.at[j], target))
                passing = relay.at[pl.ds(j * TILE, TILE)]
                for i, lat in enumerate(lats):
                    rows = pl.ds(i * TILE, TILE)
                    self.via[i].append(
                        remote(source.at[rows], passing, send.at[j], relay_sem.at[0], (lat, place.lon))
                    )
                    self.onward[i].append(
                        remote(passing, landing.at[rows], relay_sem.at[1], recv.at[j], far)
                    )
            self.passing = remote(relay, relay, relay_sem.at[1], relay_sem.at[0], place.partner())

        def start_relayed(self):
            @pl.when(self.end)
            def _():
                for copies in self.via:
                    for copy in copies:
                        copy.start()

        def start(self):
            @pl.when(jnp.logical_and(self.sends, jnp.logical_not(self.end)))
            def _():
                for copy in self.direct:
                    copy.start()

        def pass_on(self):
            is_relay = functools.reduce(jnp.logical_or, [place.lat == lat for lat in self.lats])

            @pl.when(is_relay)
            def _():
                self.passing.wait_recv()

            for lat, copies in zip(self.lats, self.onward):
                @pl.when(place.lat == lat)
                def _():
                    for copy in copies:
                        copy.start()

        def wait_recv(self):
            @pl.when(self.receives)
            def _():
                for copy in self.direct:
                    copy.wait_recv()

        def wait_send(self):
            @pl.when(self.sends)
            def _():
                for copy in self.direct:
                    copy.wait_send()

            is_relay = functools.reduce(jnp.logical_or, [place.lat == lat for lat in self.lats])

            @pl.when(is_relay)
            def _():
                self.passing.wait_send()

    back, side_back = r.back, r.side_back
    last_rows = pl.ds(half_rows, half_rows)
    rows_out = Crossing(
        [tok.at[last_rows], cot.at[last_rows]], [r.row_tok, r.row_cot], relays.out_rows, relays.low_end,
        not_last, not_first, (place.lat + 1, place.lon), (relays.first_high, place.lon),
        r.out_send, r.out_recv, r.relay, r.relay_sem,
    )
    corner_out = Crossing(
        [packed.at[1]], [side.at[1]], relays.out_corner, relays.low_end,
        not_last, not_first, (place.lat + 1, place.east()), (relays.first_high, place.east()),
        r.corner_send, r.corner_recv, r.corner, r.corner_sem,
    )
    rows_back = Crossing(
        [back.at[last_rows]], [r.row_back], relays.back_rows, relays.high_end,
        not_first, not_last, (place.lat - 1, place.lon), (relays.last_low, place.lon),
        r.back_send, r.back_recv, r.relay_back, r.relay_back_sem,
    )
    corner_back = Crossing(
        [back.at[pl.ds(2 * half_rows + 32, 32)]], [side_back.at[1]], relays.back_corner, relays.high_end,
        not_first, not_last, (place.lat - 1, place.west()), (relays.last_low, place.west()),
        r.corner_back_send, r.corner_back_recv, r.corner_back, r.corner_back_sem,
    )
    side_return = remote(
        back.at[pl.ds(2 * half_rows, 32)], side_back.at[0], halo_send.at[1], halo_recv.at[1],
        (place.lat, place.west()),
    )

    def send_relayed():
        rows_out.start_relayed()
        corner_out.start_relayed()

    def send_halos():
        rows_out.start()
        corner_out.start()
        side_copy.start()

    def pass_on():
        rows_out.pass_on()
        corner_out.pass_on()

    blocks = r.blocks

    def tile_at(n):
        which, group = divmod(n, groups)
        return group, pl.ds(which * width, width)

    def join_ring():
        ring_all.wait_recv()

        for pair in range(lons // 2):
            tiles = [[], [], []]
            for z_hi in range(Z_HI):
                even = units[z_hi * lons + 2 * pair].astype(F32)
                odd = units[z_hi * lons + 2 * pair + 1].astype(F32)
                turned_top = pltpu.roll(odd[0:8], 64, 1)
                turned_low = pltpu.roll(odd[8:16], 64, 1)
                tiles[0].append(even[0:8])
                tiles[1].append(jnp.where(lane_of < 64, even[8:16], turned_top))
                tiles[2].append(jnp.where(lane_of < 64, turned_top, turned_low))
            for j in range(3):
                group, lanes = tile_at(pair * 3 + j)
                blocks[group, place.core, place.p, :, lanes] = jnp.concatenate(tiles[j], axis=0).astype(BF16)

    def plane_copy(group, k):
        own = blocks.at[group, place.core, place.p]
        return remote(
            own, own, r.plane_send.at[group], r.plane_recv.at[group], place.plane_at(place.plane_index(k))
        )

    def plane_all(group):
        others = blocks.at[group, place.core, pl.ds(0, planes - 1)]
        return remote(others, others, r.plane_send.at[group], r.plane_recv.at[group], place.partner())

    def core_copy(group):
        block = blocks.at[group, place.core]
        return remote(block, block, r.core_send.at[group], r.core_recv.at[group], place.partner())

    def core_arrival(group):
        block = blocks.at[group, 1 - place.core]
        return remote(block, block, r.core_send.at[group], r.core_recv.at[group], place.partner())

    def send_blocks(group):
        @pl.loop(1, planes)
        def _(k):
            plane_copy(group, k).start()

    own_count = r.counts[place.lat]
    previous = jnp.where(not_first, r.counts[jnp.maximum(place.lat - 1, 0)], 0)
    row_of = r.row_of[...]
    limit = jnp.where(row_of < SHIFT_ROWS, previous - SHIFT_ROWS, own_count + SHIFT_ROWS)
    valid = jnp.where(row_of < jnp.minimum(limit, WIN_ROWS), 1.0, 0.0)
    take_own, take_row, take_side = r.take_own, r.take_row, r.take_side

    def framed_of(own, row, first):
        return (
            jnp.dot(take_own[...], own[...], preferred_element_type=F32)
            + jnp.dot(take_row[...], row[...], preferred_element_type=F32)
            + jnp.dot(take_side[first], side[0], preferred_element_type=F32)
            + jnp.dot(take_side[first + 1], side[1], preferred_element_type=F32)
        )

    hidden, normed, spread, out_grad = r.hidden, r.normed, r.spread, r.out_grad
    def frame():
        rows_out.wait_recv()
        corner_out.wait_recv()
        side_copy.wait_recv()

        framed = framed_of(tok, r.row_tok, 0)
        center = framed - jnp.mean(framed, axis=-1, keepdims=True)
        inverse = lax.rsqrt(jnp.mean(center * center, axis=-1, keepdims=True) + EPSILON)
        normal = center * inverse
        normed[...] = normal
        spread[...] = jnp.broadcast_to(inverse, spread.shape)
        hidden[...] = normal.astype(BF16)
        r.turned_hidden[...] = normal.astype(BF16).T
        framed = framed_of(cot, r.row_cot, 2)
        for j in range(features // 128):
            lanes = slice(j * 128, j * 128 + 128)
            out_grad[:, lanes] = jnp.where(valid > 0.0, framed[:, lanes], 0.0).astype(BF16)

    weight, qkv, qkv_grad = r.weight, r.qkv, r.qkv_grad

    def forward_arrivals(group):
        plane_all(group).wait_recv()
        core_copy(group).start()

    def collect(group):
        core_arrival(group).wait_recv()
        for p in range(planes):
            first = blocks[group, 0, p].astype(F32)
            second = blocks[group, 1, p].astype(F32)
            for z_hi in range(Z_HI):
                take = slice(z_hi * 8, z_hi * 8 + 8)
                rows = pl.ds((z_hi * planes + p) * 16, 16)
                weight[group, rows, :] = jnp.concatenate([first[take], second[take]], axis=0).astype(BF16)

    factor = HEAD_DIM ** (-0.5)
    whole, rest = divmod(GROUP * PAD, 128)
    allowed = jnp.concatenate([valid[0:PAD]] * whole + [valid[0:PAD, 0:rest]], axis=1) > 0.0
    mask = r.head_mask[...]
    windows = hidden.shape[0] // PAD

    def project(group):
        qkv[group] = jnp.dot(hidden[...], weight[group], preferred_element_type=F32).astype(BF16)

    def attend(group):
        for window in range(windows):
            at = slice(window * PAD, window * PAD + PAD)
            lanes = [slice(j * width, (j + 1) * width) for j in range(3)]
            query, keyed, valued = (qkv[group, at, lane] for lane in lanes)
            grad = out_grad[at, group * width : (group + 1) * width]
            query = jnp.concatenate([query] * GROUP, axis=0) * mask
            grad = jnp.concatenate([grad] * GROUP, axis=0) * mask
            scores = contract(keyed, query, ((1,), (1,))) * factor
            scores = jnp.where(allowed, scores, -1000000000.0)
            exponent = jnp.exp(scores - jnp.max(scores, axis=0, keepdims=True))
            probs = exponent * (1.0 / jnp.sum(exponent, axis=0, keepdims=True))
            weight_grad = contract(valued, grad, ((1,), (1,)))
            mixed = jnp.sum(probs * weight_grad, axis=0, keepdims=True)
            score_grad = (probs * (weight_grad - mixed) * factor).astype(BF16)
            value_grad = jnp.dot(probs.astype(BF16), grad, preferred_element_type=F32)
            key_grad = jnp.dot(score_grad, query, preferred_element_type=F32)
            turned = contract(score_grad, keyed, ((0,), (0,)))
            query_grad = turned[0:PAD] * mask[0:PAD].astype(F32)
            for h in range(1, GROUP):
                rows_h = slice(h * PAD, h * PAD + PAD)
                query_grad = query_grad + turned[rows_h] * mask[rows_h].astype(F32)
            for lane, value in zip(lanes, (query_grad, key_grad, value_grad)):
                qkv_grad[group, at, lane] = value.astype(BF16)

    part = r.part

    def weigh(group):
        for j in range(3):
            lanes = slice(j * width, (j + 1) * width)
            piece = jnp.dot(r.turned_hidden[...], qkv_grad[group, :, lanes], preferred_element_type=F32)
            for core in range(CORES):
                for p in range(planes):
                    first = (p * CORES + core) * 8
                    both = [piece[z * planes * CORES * 8 + first :][0:8] for z in range(Z_HI)]
                    part[group, core, p, :, lanes] = jnp.concatenate(both, axis=0).astype(BF16)

    from_core, sums, from_plane, total = r.from_core, r.sums, r.from_plane, r.total

    def core_part(group):
        return remote(
            part.at[group, 1 - place.core], from_core.at[group],
            r.core_part_send.at[group], r.core_part_recv.at[group], place.partner(),
        )

    def plane_part(group, k):
        p = place.plane_index(k)
        return remote(
            sums.at[group, p], from_plane.at[group, place.p],
            r.plane_part_send.at[group], r.plane_part_recv.at[group], place.plane_at(p),
        )

    def plane_part_all(group):
        others = pl.ds(0, planes - 1)
        return remote(
            sums.at[group, others], from_plane.at[group, others],
            r.plane_part_send.at[group], r.plane_part_recv.at[group], place.partner(),
        )

    def send_core(group):
        core_part(group).start()

    def send_plane(group):
        core_part(group).wait_recv()
        sums[group] = (part[group, place.core].astype(F32) + from_core[group].astype(F32)).astype(BF16)

        @pl.loop(1, planes)
        def _(k):
            plane_part(group, k).start()

        from_plane[group, place.p] = sums[group, place.p]

    def add_plane(group):
        plane_part_all(group).wait_recv()
        total[group] = jnp.sum(from_plane[group].astype(F32), axis=0)

    def accumulate(group):
        term = contract(qkv_grad[group], weight[group], ((1,), (1,)))
        if group == 0:
            r.hidden_grad[...] = term
        else:
            r.hidden_grad[...] += term

    def differentiate():
        hidden_grad = r.hidden_grad[...]
        normal = normed[...]
        mean_grad = jnp.mean(hidden_grad, axis=-1, keepdims=True)
        mean_mixed = jnp.mean(hidden_grad * normal, axis=-1, keepdims=True)
        frame_grad = spread[...] * (hidden_grad - mean_grad - normal * mean_mixed)
        back[...] = jnp.dot(r.give[...], frame_grad.astype(BF16), preferred_element_type=F32).astype(BF16)

    def return_relayed():
        rows_back.start_relayed()
        corner_back.start_relayed()

    def return_halos():
        rows_back.start()
        corner_back.start()
        side_return.start()

    def pass_back():
        rows_back.pass_on()
        corner_back.pass_on()

    part_units, from_ring = r.part_units, r.from_ring

    def ring_part(k):
        z = place.ring_index(k)
        return remote(
            part_units.at[z], from_ring.at[place.z], r.ring_part_send.at[0], r.ring_part_recv.at[0],
            place.ring_at(z),
        )

    ring_part_all = remote(
        part_units.at[others], from_ring.at[others], r.ring_part_send.at[0], r.ring_part_recv.at[0],
        place.partner(),
    )

    def send_ring_parts():
        for pair in range(lons // 2):
            for z_hi in range(Z_HI):
                tiles = []
                for j in range(3):
                    group, lanes = tile_at(pair * 3 + j)
                    tiles.append(total[group, pl.ds(z_hi * 8, 8), lanes])
                turned = [pltpu.roll(tile, 64, 1) for tile in tiles]
                part_units[z_hi * lons + 2 * pair] = jnp.concatenate([tiles[0], tiles[1]], axis=0).astype(BF16)
                part_units[z_hi * lons + 2 * pair + 1] = jnp.concatenate(
                    [jnp.where(lane_of < 64, turned[1], turned[2]), turned[2]], axis=0
                ).astype(BF16)

        @pl.loop(0, rings - 1)
        def _(k):
            ring_part(far_first(k, rings)).start()

        from_ring[place.z] = part_units[place.z]

    def finish_tokens():
        rows_back.wait_recv()
        corner_back.wait_recv()
        side_return.wait_recv()

        for part_of in range(2):
            rows = pl.ds(part_of * half_rows, half_rows)
            inner = back[0:half_rows] if part_of == 0 else r.row_back[...]
            outer = jnp.dot(r.place_sel[...], side_back[part_of], preferred_element_type=F32)
            returned[rows] = (inner.astype(F32) + outer).astype(BF16)

    def finish_weight():
        ring_part_all.wait_recv()

        result = from_ring[0].astype(F32)
        for z in range(1, rings):
            result = result + from_ring[z].astype(F32)
        weight_gradient[:, 0:128] = result[0:8]
        weight_gradient[:, 128:192] = result[8:16, 0:64]

    def drain():
        rows_out.wait_send()
        rows_back.wait_send()
        corner_out.wait_send()
        corner_back.wait_send()
        side_copy.wait_send()
        side_return.wait_send()
        ring_all.wait_send()
        ring_part_all.wait_send()
        for group in range(groups):
            plane_all(group).wait_send()
            plane_part_all(group).wait_send()
            core_copy(group).wait_send()
            core_part(group).wait_send()

    send_relayed()
    send_ring()
    send_halos()
    pass_on()
    join_ring()
    for group in range(groups):
        send_blocks(group)
    frame()
    forward_arrivals(0)
    for group in range(groups):
        collect(group)
        project(group)
        attend(group)
        if group > 0:
            send_plane(group - 1)
        if group < groups - 1:
            forward_arrivals(group + 1)
        weigh(group)
        send_core(group)
        accumulate(group)
    differentiate()
    return_relayed()
    send_plane(groups - 1)
    return_halos()
    for group in range(groups - 1):
        add_plane(group)
    pass_back()
    add_plane(groups - 1)
    send_ring_parts()
    finish_tokens()
    finish_weight()
    drain()


def frame_tables(cols):
    windows = cols // WIN_COLS
    total = windows * PAD
    half = SHIFT_ROWS * cols
    own = np.zeros((total, 2 * half), np.float32)
    row = np.zeros((total, half), np.float32)
    side = np.zeros((4, total, 48), np.float32)
    give = np.zeros((2 * half + 64, total), np.float32)
    row_of = np.full((total, 128), WIN_ROWS, np.int32)
    for window in range(windows):
        for r in range(WIN_ROWS):
            for c in range(WIN_COLS):
                t = window * PAD + r * WIN_COLS + c
                row_of[t] = r
                rr, g = r - SHIFT_ROWS, window * WIN_COLS + c - SHIFT_COLS
                upper = rr < 0
                if g >= 0:
                    if upper:
                        row[t, r * cols + g] = 1
                        give[half + r * cols + g, t] = 1
                    else:
                        own[t, rr * cols + g] = 1
                        give[rr * cols + g, t] = 1
                else:
                    at = (r % SHIFT_ROWS) * SHIFT_COLS + g + SHIFT_COLS
                    side[int(upper), t, at] = 1
                    side[2 + int(upper), t, 18 + at] = 1
                    give[2 * half + 32 * int(upper) + at, t] = 1
    return own, row, side, give, row_of


def on_device(lats, lons, tokens, cotangent, qkv_weight, band_rows):
    features = tokens.shape[-1]
    tok = tokens.reshape(-1, features)
    cot = cotangent.reshape(-1, features)
    count = tok.shape[0]
    half = count // 2
    cols = half // SHIFT_ROWS
    planes, rings = Y * X, Z_HI * lons
    columns = qkv_weight.shape[1] * lons
    width = GROUP * HEAD_DIM
    groups = features // width
    take_own, take_row, take_side, give, row_of = frame_tables(cols)
    total = take_own.shape[0]
    sel = np.zeros((2, 48, half), np.float32)
    place_sel = np.zeros((half, 32), np.float32)
    for row in range(SHIFT_ROWS):
        for col in range(SHIFT_COLS):
            at, edge = row * SHIFT_COLS + col, row * cols + cols - SHIFT_COLS + col
            sel[0, at, edge] = 1
            sel[1, 18 + at, edge] = 1
            place_sel[edge, at] = 1
    head_mask = np.zeros((GROUP, PAD, GROUP, HEAD_DIM), np.float32)
    for h in range(GROUP):
        head_mask[h, :, h] = 1
    low = lambda table: jnp.asarray(table, BF16)
    loaded = dict(
        w_in=qkv_weight, counts=band_rows, tok=tok, cot=cot, sel=low(sel), row_of=jnp.asarray(row_of), take_own=low(take_own), take_row=low(take_row),
        take_side=low(take_side), head_mask=low(head_mask.reshape(GROUP * PAD, width)), give=low(give),
        place_sel=low(place_sel),
    )
    dma = pltpu.SemaphoreType.DMA
    scratch = {name: VMEM(array.shape, array.dtype) for name, array in loaded.items()}
    scratch.update(counts=pltpu.SMEM(band_rows.shape, band_rows.dtype))
    scratch.update(
        wide=VMEM((8, 256), F32),
        unit=VMEM((16, 128), BF16),
        units=VMEM((rings, 16, 128), BF16),
        blocks=VMEM((groups, CORES, planes, 16, columns // groups), BF16),
        packed=VMEM((2, 48, features), BF16),
        side=VMEM((2, 48, features), BF16),
        row_tok=VMEM((half, features), BF16),
        row_cot=VMEM((half, features), BF16),
        relay=VMEM((2 * TILE, features), BF16),
        corner=VMEM((TILE, features), BF16),
        relay_back=VMEM((TILE, features), BF16),
        corner_back=VMEM((TILE, features), BF16),
        weight=VMEM((groups, features, columns // groups), BF16),
        hidden=VMEM((total, features), BF16),
        turned_hidden=VMEM((features, total), BF16),
        normed=VMEM((total, features), F32),
        spread=VMEM((total, features), F32),
        hidden_grad=VMEM((total, features), F32),
        out_grad=VMEM((total, features), BF16),
        qkv=VMEM((groups, total, columns // groups), BF16),
        qkv_grad=VMEM((groups, total, columns // groups), BF16),
        part=VMEM((groups, CORES, planes, 16, columns // groups), BF16),
        from_core=VMEM((groups, planes, 16, columns // groups), BF16),
        sums=VMEM((groups, planes, 16, columns // groups), BF16),
        from_plane=VMEM((groups, planes, 16, columns // groups), BF16),
        total=VMEM((groups, 16, columns // groups), F32),
        back=VMEM(give.shape[:1] + (features,), BF16),
        row_back=VMEM((half, features), BF16),
        side_back=VMEM((2, 32, features), BF16),
        part_units=VMEM((rings, 16, 128), BF16),
        from_ring=VMEM((rings, 16, 128), BF16),
        load_sem=dma((len(loaded),)),
        relay_sem=dma((2,)),
        corner_sem=dma((2,)),
        relay_back_sem=dma((2,)),
        corner_back_sem=dma((2,)),
    )
    both = dict(
        ring=(1,), plane=(groups,), core=(groups,), halo=(2,), out=(2,),
        corner=(1,), back=(1,), corner_back=(1,), core_part=(groups,), plane_part=(groups,), ring_part=(1,),
    )
    for name, shape in both.items():
        scratch[name + "_send"] = dma(shape)
        scratch[name + "_recv"] = dma(shape)
    returned, weight_gradient = pl.pallas_call(
        functools.partial(kernel, lats, lons, len(loaded), list(scratch)),
        out_shape=(
            jax.ShapeDtypeStruct(tok.shape, BF16),
            jax.ShapeDtypeStruct(qkv_weight.shape, F32),
        ),
        in_specs=[pl.BlockSpec(memory_space=pl.ANY)] * len(loaded),
        out_specs=[pl.BlockSpec(memory_space=VMEM)] * 2,
        scratch_shapes=list(scratch.values()),
        compiler_params=pltpu.CompilerParams(
            collective_id=0, has_side_effects=True, vmem_limit_bytes=56 * 2**20
        ),
        name="sub_block",
    )(*loaded.values())
    token_grad = cotangent.astype(F32) + returned.reshape(tokens.shape).astype(F32)
    return token_grad.astype(BF16), weight_gradient


def solution(mesh):
    return jax.shard_map(
        functools.partial(on_device, mesh.shape["lat"], mesh.shape["lon"]),
        mesh=mesh,
        in_specs=(P("lat", "lon", None), P("lat", "lon", None), P("lat", "lon"), P()),
        out_specs=(P("lat", "lon", None), P("lat", "lon")),
        check_vma=False,
    )
```

time: 70.3 us -> 63 us (0.90)
  Pallas kernels: 66 us -> 58.9 us
  other arithmetic: 0 us -> 1.76 us
  local copies, waits for them, and re-layouts: 2.3 us -> 0.61 us
    pallas_call x1, Pallas kernels: 66 us -> 58.9 us  [on_device(): pl.pallas_call(functools.partial(kernel, lats, lons, len(loaded), list(sc...]
    convert_element_type x0 -> x1, other arithmetic: none -> 1.76 us  [on_device(): return (token_grad.astype(BF16), weight_gradient)]
    unnamed x4 -> x5, local copies, waits for them, and re-layouts: 2.3 us -> 0.61 us
where the time goes in v4:
time: 63 us; the launch traced here: 61.9 us
  Pallas kernels  58.9 us (93%)
  other arithmetic  1.76 us (3%)
  between operations  0.66 us (1%)
    pallas_call x1, Pallas kernels, on_device(): pl.pallas_call(functools.partial(kernel, lats, lons, len(loaded), list(sc...  58.9 us
    convert_element_type x1, other arithmetic, on_device(): return (token_grad.astype(BF16), weight_gradient)  1.76 us

profile of v4, /device:TPU:6, one launch (start us, length us, event | category | flops | bytes accessed | tf_op | source)
XLA Modules:
  0.0 61.9 jit_solution(17451458548976335928)
XLA Ops:
  0.6 0.0 copy-start
  0.6 58.9 %sub_block.1 = (bf16[288,512]{1,0:T(8,128)(2,1)}, f32[8,192]{1,0:T(8,128)}) custom-call(bf16[8,192]{1,0:T(8,128)(2,1)} %refs_0_.1, s32[64]{0:T(128)} %refs_1_.1, bf16[288,512]{1,0:T(8,128)(2,1)} %bitcast.6, bf16[288,512]{1,0:T(8,128)(2,1)} %bitcast.4, bf16[2,48,144]{2,1,0:T(8,128)(2,1)} %constant.16.clone.refs_4_, s32[320,128]{1,0:T(8,128)} %constant.17.clone.refs_5_, ...), custom_call_target="tpu_custom_call" | custom-call | tf_op jit(solution)/shard_map/sub_block/pallas_call | solution.py:751
  59.5 0.0 copy-done
  59.5 0.0 copy-start.1
  59.5 1.8 %fusion = bf16[6,48,512]{2,1,0:T(8,128)(2,1)} fusion(bf16[6,48,512]{2,1,0:T(8,128)(2,1)} %bitcast.5, bf16[6,48,512]{2,1,0:T(8,128)(2,1)S(1)} %copy-done), kind=kLoop, calls=%fused_computation.1 | loop fusion | flops 589824 | bytes 884736 | tf_op jit(solution)/shard_map/convert_element_type | solution.py:766
  61.3 0.0 copy-done.1
  61.3 0.6 copy.15
Async XLA Ops:
  0.6 58.9 %copy-start = (bf16[6,48,512]{2,1,0:T(8,128)(2,1)S(1)}, bf16[6,48,512]{2,1,0:T(8,128)(2,1)}, u32[]{:S(2)}) copy-start(bf16[6,48,512]{2,1,0:T(8,128)(2,1)} %param.13) | copy-start | bytes 884740
  59.5 1.8 %copy-start.1 = (f32[8,192]{1,0:T(8,128)S(1)}, f32[8,192]{1,0:T(8,128)}, u32[]{:S(2)}) copy-start(f32[8,192]{1,0:T(8,128)} %get-tuple-element.9) | copy-start | bytes 18436

commit v5 on v4

--- a/solution.py
+++ b/solution.py
@@ -35,20 +35,19 @@
         self.p = lax.div(lax.rem(self.lat, self.planes * CORES), CORES)
         self.core = lax.rem(self.lat, CORES)
         self.z = self.z_hi * lons + self.lon
-
-    def ring_at(self, z):
-        return (lax.div(z, self.lons) * self.planes * CORES + self.p * CORES + self.core, lax.rem(z, self.lons))
-
-    def plane_at(self, p):
-        return (self.z_hi * self.planes * CORES + p * CORES + self.core, self.lon)
-
-    def ring_index(self, k):
-        return lax.rem(self.z + k, self.rings)
-
-    def plane_index(self, k):
-        x = lax.rem(lax.rem(self.p, X) + lax.rem(k, X), X)
-        y = lax.rem(lax.div(self.p, X) + lax.div(k, X), Y)
-        return y * X + x
+        self.ring = [None] + [self._ring(k) for k in range(1, self.rings)]
+        self.plane = [None] + [self._plane(k) for k in range(1, self.planes)]
+
+    def _ring(self, k):
+        z = lax.rem(self.z + k, self.rings)
+        lat = lax.div(z, self.lons) * self.planes * CORES + self.p * CORES + self.core
+        return z, (lat, lax.rem(z, self.lons))
+
+    def _plane(self, k):
+        x = lax.rem(lax.rem(self.p, X) + k % X, X)
+        y = lax.rem(lax.div(self.p, X) + k // X, Y)
+        p = y * X + x
+        return p, (self.z_hi * self.planes * CORES + p * CORES + self.core, self.lon)
 
     def partner(self):
         return (self.lat + 1 - 2 * self.core, self.lon)
@@ -98,9 +97,8 @@
         self.back_rows, self.back_corner = high(BACK_ROWS), high(BACK_CORNER)
 
 
-def far_first(k, count):
-    half = count // 2
-    return half + (1 - 2 * lax.rem(k, 2)) * lax.div(k + 1, 2)
+def far_first(count):
+    return sorted(range(1, count), key=lambda k: -min(k, count - k))
 
 
 def announce(place, relays):
@@ -139,13 +137,11 @@
 
     count = count + jnp.where(above, 2, 0) + jnp.where(below, 2, 0)
 
-    @pl.loop(0, place.rings - 1)
-    def _(k):
-        signal(place.ring_at(place.ring_index(far_first(k, place.rings))))
-
-    @pl.loop(1, place.planes)
-    def _(k):
-        signal(place.plane_at(place.plane_index(k)))
+    for k in far_first(place.rings):
+        signal(place.ring[k][1])
+
+    for k in range(1, place.planes):
+        signal(place.plane[k][1])
 
     signal(place.partner())
     return count
@@ -213,16 +209,15 @@
 
     def ring_copy(k):
         return remote(
-            unit, units.at[place.z], r.ring_send.at[0], r.ring_recv.at[0], place.ring_at(place.ring_index(k))
+            unit, units.at[place.z], r.ring_send.at[0], r.ring_recv.at[0], place.ring[k][1]
         )
 
     others = pl.ds(0, rings - 1)
     ring_all = remote(units.at[others], units.at[others], r.ring_send.at[0], r.ring_recv.at[0], place.partner())
 
     def send_ring():
-        @pl.loop(0, rings - 1)
-        def _(k):
-            ring_copy(far_first(k, rings)).start()
+        for k in far_first(rings):
+            ring_copy(k).start()
 
     halo_send, halo_recv = r.halo_send, r.halo_recv
     side_copy = remote(packed.at[0], side.at[0], halo_send.at[0], halo_recv.at[0], (place.lat, place.east()))
@@ -354,7 +349,7 @@
     def plane_copy(group, k):
         own = blocks.at[group, place.core, place.p]
         return remote(
-            own, own, r.plane_send.at[group], r.plane_recv.at[group], place.plane_at(place.plane_index(k))
+            own, own, r.plane_send.at[group], r.plane_recv.at[group], place.plane[k][1]
         )
 
     def plane_all(group):
@@ -370,8 +365,7 @@
         return remote(block, block, r.core_send.at[group], r.core_recv.at[group], place.partner())
 
     def send_blocks(group):
-        @pl.loop(1, planes)
-        def _(k):
+        for k in range(1, planes):
             plane_copy(group, k).start()
 
     own_count = r.counts[place.lat]
@@ -479,10 +473,10 @@
         )
 
     def plane_part(group, k):
-        p = place.plane_index(k)
+        p, device = place.plane[k]
         return remote(
             sums.at[group, p], from_plane.at[group, place.p],
-            r.plane_part_send.at[group], r.plane_part_recv.at[group], place.plane_at(p),
+            r.plane_part_send.at[group], r.plane_part_recv.at[group], device,
         )
 
     def plane_part_all(group):
@@ -499,8 +493,7 @@
         core_part(group).wait_recv()
         sums[group] = (part[group, place.core].astype(F32) + from_core[group].astype(F32)).astype(BF16)
 
-        @pl.loop(1, planes)
-        def _(k):
+        for k in range(1, planes):
             plane_part(group, k).start()
 
         from_plane[group, place.p] = sums[group, place.p]
@@ -540,10 +533,9 @@
     part_units, from_ring = r.part_units, r.from_ring
 
     def ring_part(k):
-        z = place.ring_index(k)
+        z, device = place.ring[k]
         return remote(
-            part_units.at[z], from_ring.at[place.z], r.ring_part_send.at[0], r.ring_part_recv.at[0],
-            place.ring_at(z),
+            part_units.at[z], from_ring.at[place.z], r.ring_part_send.at[0], r.ring_part_recv.at[0], device
         )
 
     ring_part_all = remote(
@@ -564,11 +556,13 @@
                     [jnp.where(lane_of < 64, turned[1], turned[2]), turned[2]], axis=0
                 ).astype(BF16)
 
-        @pl.loop(0, rings - 1)
-        def _(k):
-            ring_part(far_first(k, rings)).start()
+        for k in far_first(rings):
+            ring_part(k).start()
 
         from_ring[place.z] = part_units[place.z]
+
+    returned_copy = pltpu.make_async_copy(r.returned, returned, r.store_sem.at[0])
+    weight_copy = pltpu.make_async_copy(r.weight_gradient, weight_gradient, r.store_sem.at[1])
 
     def finish_tokens():
         rows_back.wait_recv()
@@ -579,7 +573,8 @@
             rows = pl.ds(part_of * half_rows, half_rows)
             inner = back[0:half_rows] if part_of == 0 else r.row_back[...]
             outer = jnp.dot(r.place_sel[...], side_back[part_of], preferred_element_type=F32)
-            returned[rows] = (inner.astype(F32) + outer).astype(BF16)
+            r.returned[rows] = (inner.astype(F32) + outer).astype(BF16)
+        returned_copy.start()
 
     def finish_weight():
         ring_part_all.wait_recv()
@@ -587,10 +582,13 @@
         result = from_ring[0].astype(F32)
         for z in range(1, rings):
             result = result + from_ring[z].astype(F32)
-        weight_gradient[:, 0:128] = result[0:8]
-        weight_gradient[:, 128:192] = result[8:16, 0:64]
+        r.weight_gradient[:, 0:128] = result[0:8]
+        r.weight_gradient[:, 128:192] = result[8:16, 0:64]
+        weight_copy.start()
 
     def drain():
+        returned_copy.wait()
+        weight_copy.wait()
         rows_out.wait_send()
         rows_back.wait_send()
         corner_out.wait_send()
@@ -612,16 +610,17 @@
     join_ring()
     for group in range(groups):
         send_blocks(group)
+    forward_arrivals(0)
+    forward_arrivals(1)
     frame()
-    forward_arrivals(0)
     for group in range(groups):
         collect(group)
         project(group)
         attend(group)
         if group > 0:
             send_plane(group - 1)
-        if group < groups - 1:
-            forward_arrivals(group + 1)
+        if group < groups - 2:
+            forward_arrivals(group + 2)
         weigh(group)
         send_core(group)
         accumulate(group)
@@ -637,6 +636,53 @@
     finish_tokens()
     finish_weight()
     drain()
+
+
+def finish_kernel(returned, cot, weight, token_grad, weight_gradient, first, second, total, load_sem, store_sem):
+    parts = first.shape[0]
+    rows = first.shape[1]
+    weight_copy = pltpu.make_async_copy(weight, weight_gradient, store_sem.at[parts])
+    weight_copy.start()
+    loads, stores = [], []
+    for i in range(parts):
+        at = pl.ds(i * rows, rows)
+        loads.append(
+            (
+                pltpu.make_async_copy(returned.at[at], first.at[i], load_sem.at[i, 0]),
+                pltpu.make_async_copy(cot.at[at], second.at[i], load_sem.at[i, 1]),
+            )
+        )
+        stores.append(pltpu.make_async_copy(total.at[i], token_grad.at[at], store_sem.at[i]))
+    for pair in loads:
+        for load in pair:
+            load.start()
+    for i in range(parts):
+        for load in loads[i]:
+            load.wait()
+        total[i] = (second[i].astype(F32) + first[i].astype(F32)).astype(BF16)
+        stores[i].start()
+    for store in stores:
+        store.wait()
+    weight_copy.wait()
+
+
+def finish(returned, cot, weight):
+    parts = 3
+    block = VMEM((parts, cot.shape[0] // parts, cot.shape[1]), BF16)
+    return pl.pallas_call(
+        finish_kernel,
+        out_shape=(
+            jax.ShapeDtypeStruct(cot.shape, BF16),
+            jax.ShapeDtypeStruct(weight.shape, F32),
+        ),
+        in_specs=[pl.BlockSpec(memory_space=pl.ANY)] * 3,
+        out_specs=[pl.BlockSpec(memory_space=pl.ANY)] * 2,
+        scratch_shapes=[
+            block, block, block, pltpu.SemaphoreType.DMA((parts, 2)), pltpu.SemaphoreType.DMA((parts + 1,)),
+        ],
+        compiler_params=pltpu.CompilerParams(vmem_limit_bytes=56 * 2**20),
+        name="finish",
+    )(returned, cot, weight)
 
 
 def frame_tables(cols):
@@ -735,7 +781,10 @@
         side_back=VMEM((2, 32, features), BF16),
         part_units=VMEM((rings, 16, 128), BF16),
         from_ring=VMEM((rings, 16, 128), BF16),
+        returned=VMEM(tok.shape, BF16),
+        weight_gradient=VMEM(qkv_weight.shape, F32),
         load_sem=dma((len(loaded),)),
+        store_sem=dma((2,)),
         relay_sem=dma((2,)),
         corner_sem=dma((2,)),
         relay_back_sem=dma((2,)),
@@ -755,15 +804,15 @@
             jax.ShapeDtypeStruct(qkv_weight.shape, F32),
         ),
         in_specs=[pl.BlockSpec(memory_space=pl.ANY)] * len(loaded),
-        out_specs=[pl.BlockSpec(memory_space=VMEM)] * 2,
+        out_specs=[pl.BlockSpec(memory_space=pl.ANY)] * 2,
         scratch_shapes=list(scratch.values()),
         compiler_params=pltpu.CompilerParams(
             collective_id=0, has_side_effects=True, vmem_limit_bytes=56 * 2**20
         ),
         name="sub_block",
     )(*loaded.values())
-    token_grad = cotangent.astype(F32) + returned.reshape(tokens.shape).astype(F32)
-    return token_grad.astype(BF16), weight_gradient
+    token_grad, weight_gradient = finish(returned, cot, weight_gradient)
+    return token_grad.reshape(tokens.shape), weight_gradient
 
 
 def solution(mesh):

time: 63 us -> 61.7 us (0.979)
  other arithmetic: 1.76 us -> 0 us
  Pallas kernels: 58.9 us -> 60.3 us
    pallas_call x0 -> x1, Pallas kernels: none -> 1.89 us  [finish(): pl.pallas_call(finish_kernel, out_shape=(jax.ShapeDtypeStruct(cot.shape,...]
    convert_element_type x1 -> x0, other arithmetic: 1.76 us -> none  [on_device(): return (token_grad.astype(BF16), weight_gradient)]
where the time goes in v5:
time: 61.7 us; the launch traced here: 61 us
  Pallas kernels  60.3 us (98%)
  between operations  0.64 us (1%)
    pallas_call x1, Pallas kernels, on_device(): pl.pallas_call(functools.partial(kernel, lats, lons, len(loaded), list(sc...  58.5 us
    pallas_call x1, Pallas kernels, finish(): pl.pallas_call(finish_kernel, out_shape=(jax.ShapeDtypeStruct(cot.shape,...  1.89 us

profile of v5, /device:TPU:6, one launch (start us, length us, event | category | flops | bytes accessed | tf_op | source)
XLA Modules:
  0.0 61.0 jit_solution(8677358716518017521)
XLA Ops:
  0.6 58.5 %sub_block.1 = (bf16[288,512]{1,0:T(8,128)(2,1)}, f32[8,192]{1,0:T(8,128)}) custom-call(bf16[8,192]{1,0:T(8,128)(2,1)} %refs_0_.1, s32[64]{0:T(128)} %refs_1_.1, bf16[288,512]{1,0:T(8,128)(2,1)} %bitcast.5, bf16[288,512]{1,0:T(8,128)(2,1)} %bitcast.3, bf16[2,48,144]{2,1,0:T(8,128)(2,1)} %constant.16.clone.refs_4_, s32[320,128]{1,0:T(8,128)} %constant.17.clone.refs_5_, ...), custom_call_target="tpu_custom_call" | custom-call | tf_op jit(solution)/shard_map/sub_block/pallas_call | solution.py:800
  59.1 1.9 %finish.1 = (bf16[288,512]{1,0:T(8,128)(2,1)}, f32[8,192]{1,0:T(8,128)}) custom-call(bf16[288,512]{1,0:T(8,128)(2,1)} %get-tuple-element.6.returned, bf16[288,512]{1,0:T(8,128)(2,1)} %bitcast.4, f32[8,192]{1,0:T(8,128)} %get-tuple-element.7.weight), custom_call_target="tpu_custom_call" | custom-call | tf_op jit(solution)/shard_map/finish/pallas_call | solution.py:672

commit v6 on v5

--- a/solution.py
+++ b/solution.py
@@ -20,6 +20,7 @@
 SHIFT_COLS = 6
 HEAD_DIM = 32
 EPSILON = 1e-05
+LOG2_E = 1.4426950408889634
 
 Z_HI, Y, X, CORES = 2, 4, 4, 2
 
@@ -172,10 +173,9 @@
         pltpu.make_async_copy(source, target, r.load_sem.at[i])
         for i, (source, target) in enumerate(zip(sources, targets))
     ]
+    expected = announce(place, relays)
     for load in loads:
         load.start()
-
-    expected = announce(place, relays)
 
     wide, unit, units = r.wide, r.unit, r.units
     wide[...] = jnp.zeros_like(wide)
@@ -435,9 +435,8 @@
             grad = out_grad[at, group * width : (group + 1) * width]
             query = jnp.concatenate([query] * GROUP, axis=0) * mask
             grad = jnp.concatenate([grad] * GROUP, axis=0) * mask
-            scores = contract(keyed, query, ((1,), (1,))) * factor
-            scores = jnp.where(allowed, scores, -1000000000.0)
-            exponent = jnp.exp(scores - jnp.max(scores, axis=0, keepdims=True))
+            scores = jnp.where(allowed, contract(keyed, query, ((1,), (1,))), -1000000000.0 / factor)
+            exponent = jnp.exp2((scores - jnp.max(scores, axis=0, keepdims=True)) * (factor * LOG2_E))
             probs = exponent * (1.0 / jnp.sum(exponent, axis=0, keepdims=True))
             weight_grad = contract(valued, grad, ((1,), (1,)))
             mixed = jnp.sum(probs * weight_grad, axis=0, keepdims=True)
@@ -464,6 +463,7 @@
                     both = [piece[z * planes * CORES * 8 + first :][0:8] for z in range(Z_HI)]
                     part[group, core, p, :, lanes] = jnp.concatenate(both, axis=0).astype(BF16)
 
+    spans = ((0, 1), (1, 2), (2, 3), (3, 4))
     from_core, sums, from_plane, total = r.from_core, r.sums, r.from_plane, r.total
 
     def core_part(group):
@@ -472,35 +472,37 @@
             r.core_part_send.at[group], r.core_part_recv.at[group], place.partner(),
         )
 
-    def plane_part(group, k):
+    def plane_part(first, last, k):
         p, device = place.plane[k]
+        span = pl.ds(first, last - first)
         return remote(
-            sums.at[group, p], from_plane.at[group, place.p],
-            r.plane_part_send.at[group], r.plane_part_recv.at[group], device,
+            sums.at[p, span], from_plane.at[place.p, span],
+            r.plane_part_send.at[first], r.plane_part_recv.at[first], device,
         )
 
-    def plane_part_all(group):
-        others = pl.ds(0, planes - 1)
+    def plane_part_all(first, last):
+        others, span = pl.ds(0, planes - 1), pl.ds(first, last - first)
         return remote(
-            sums.at[group, others], from_plane.at[group, others],
-            r.plane_part_send.at[group], r.plane_part_recv.at[group], place.partner(),
+            sums.at[others, span], from_plane.at[others, span],
+            r.plane_part_send.at[first], r.plane_part_recv.at[first], place.partner(),
         )
 
     def send_core(group):
         core_part(group).start()
 
-    def send_plane(group):
-        core_part(group).wait_recv()
-        sums[group] = (part[group, place.core].astype(F32) + from_core[group].astype(F32)).astype(BF16)
-
+    def send_plane(first, last):
+        for group in range(first, last):
+            core_part(group).wait_recv()
+            sums[:, group] = (part[group, place.core].astype(F32) + from_core[group].astype(F32)).astype(BF16)
         for k in range(1, planes):
-            plane_part(group, k).start()
-
-        from_plane[group, place.p] = sums[group, place.p]
-
-    def add_plane(group):
-        plane_part_all(group).wait_recv()
-        total[group] = jnp.sum(from_plane[group].astype(F32), axis=0)
+            plane_part(first, last, k).start()
+        for group in range(first, last):
+            from_plane[place.p, group] = sums[place.p, group]
+
+    def add_plane(first, last):
+        plane_part_all(first, last).wait_recv()
+        for group in range(first, last):
+            total[group] = jnp.sum(from_plane[:, group].astype(F32), axis=0)
 
     def accumulate(group):
         term = contract(qkv_grad[group], weight[group], ((1,), (1,)))
@@ -599,9 +601,10 @@
         ring_part_all.wait_send()
         for group in range(groups):
             plane_all(group).wait_send()
-            plane_part_all(group).wait_send()
             core_copy(group).wait_send()
             core_part(group).wait_send()
+        for first, last in spans:
+            plane_part_all(first, last).wait_send()
 
     send_relayed()
     send_ring()
@@ -618,31 +621,32 @@
         project(group)
         attend(group)
         if group > 0:
-            send_plane(group - 1)
+            send_plane(*spans[group - 1])
         if group < groups - 2:
             forward_arrivals(group + 2)
         weigh(group)
         send_core(group)
+    for group in range(groups):
         accumulate(group)
     differentiate()
     return_relayed()
-    send_plane(groups - 1)
+    send_plane(*spans[3])
     return_halos()
-    for group in range(groups - 1):
-        add_plane(group)
     pass_back()
-    add_plane(groups - 1)
+    for span in spans:
+        add_plane(*span)
     send_ring_parts()
     finish_tokens()
     finish_weight()
     drain()
 
 
-def finish_kernel(returned, cot, weight, token_grad, weight_gradient, first, second, total, load_sem, store_sem):
+def finish_kernel(returned, cot, weight, token_grad, weight_gradient, first, second, total, held, load_sem, store_sem):
     parts = first.shape[0]
     rows = first.shape[1]
-    weight_copy = pltpu.make_async_copy(weight, weight_gradient, store_sem.at[parts])
-    weight_copy.start()
+    weight_load = pltpu.make_async_copy(weight, held, store_sem.at[parts])
+    weight_store = pltpu.make_async_copy(held, weight_gradient, store_sem.at[parts + 1])
+    weight_load.start()
     loads, stores = [], []
     for i in range(parts):
         at = pl.ds(i * rows, rows)
@@ -656,6 +660,8 @@
     for pair in loads:
         for load in pair:
             load.start()
+    weight_load.wait()
+    weight_store.start()
     for i in range(parts):
         for load in loads[i]:
             load.wait()
@@ -663,7 +669,7 @@
         stores[i].start()
     for store in stores:
         store.wait()
-    weight_copy.wait()
+    weight_store.wait()
 
 
 def finish(returned, cot, weight):
@@ -678,7 +684,8 @@
         in_specs=[pl.BlockSpec(memory_space=pl.ANY)] * 3,
         out_specs=[pl.BlockSpec(memory_space=pl.ANY)] * 2,
         scratch_shapes=[
-            block, block, block, pltpu.SemaphoreType.DMA((parts, 2)), pltpu.SemaphoreType.DMA((parts + 1,)),
+            block, block, block, VMEM(weight.shape, F32),
+            pltpu.SemaphoreType.DMA((parts, 2)), pltpu.SemaphoreType.DMA((parts + 2,)),
         ],
         compiler_params=pltpu.CompilerParams(vmem_limit_bytes=56 * 2**20),
         name="finish",
@@ -773,8 +780,8 @@
         qkv_grad=VMEM((groups, total, columns // groups), BF16),
         part=VMEM((groups, CORES, planes, 16, columns // groups), BF16),
         from_core=VMEM((groups, planes, 16, columns // groups), BF16),
-        sums=VMEM((groups, planes, 16, columns // groups), BF16),
-        from_plane=VMEM((groups, planes, 16, columns // groups), BF16),
+        sums=VMEM((planes, groups, 16, columns // groups), BF16),
+        from_plane=VMEM((planes, groups, 16, columns // groups), BF16),
         total=VMEM((groups, 16, columns // groups), F32),
         back=VMEM(give.shape[:1] + (features,), BF16),
         row_back=VMEM((half, features), BF16),

time: 61.7 us -> 61.1 us (level)
    pallas_call x1, Pallas kernels: 58.5 us -> 57.8 us  [on_device(): pl.pallas_call(functools.partial(kernel, lats, lons, len(loaded), list(sc...]
where the time goes in v6:
time: 61.1 us; the launch traced here: 60.3 us
  Pallas kernels  59.7 us (98%)
  between operations  0.64 us (1%)
    pallas_call x1, Pallas kernels, on_device(): pl.pallas_call(functools.partial(kernel, lats, lons, len(loaded), list(sc...  57.8 us
    pallas_call x1, Pallas kernels, finish(): pl.pallas_call(finish_kernel, out_shape=(jax.ShapeDtypeStruct(cot.shape,...  1.91 us

profile of v6, /device:TPU:6, one launch (start us, length us, event | category | flops | bytes accessed | tf_op | source)
XLA Modules:
  0.0 60.3 jit_solution(401123590021358584)
XLA Ops:
  0.6 57.8 %sub_block.1 = (bf16[288,512]{1,0:T(8,128)(2,1)}, f32[8,192]{1,0:T(8,128)}) custom-call(bf16[8,192]{1,0:T(8,128)(2,1)} %refs_0_.1, s32[64]{0:T(128)} %refs_1_.1, bf16[288,512]{1,0:T(8,128)(2,1)} %bitcast.5, bf16[288,512]{1,0:T(8,128)(2,1)} %bitcast.3, bf16[2,48,144]{2,1,0:T(8,128)(2,1)} %constant.16.clone.refs_4_, s32[320,128]{1,0:T(8,128)} %constant.17.clone.refs_5_, ...), custom_call_target="tpu_custom_call" | custom-call | tf_op jit(solution)/shard_map/sub_block/pallas_call | solution.py:807
  58.4 1.9 %finish.1 = (bf16[288,512]{1,0:T(8,128)(2,1)}, f32[8,192]{1,0:T(8,128)}) custom-call(bf16[288,512]{1,0:T(8,128)(2,1)} %get-tuple-element.6.returned, bf16[288,512]{1,0:T(8,128)(2,1)} %bitcast.4, f32[8,192]{1,0:T(8,128)} %get-tuple-element.7.weight), custom_call_target="tpu_custom_call" | custom-call | tf_op jit(solution)/shard_map/finish/pallas_call | solution.py:678

commit v7 on v6

--- a/solution.py
+++ b/solution.py
@@ -37,7 +37,7 @@
         self.core = lax.rem(self.lat, CORES)
         self.z = self.z_hi * lons + self.lon
         self.ring = [None] + [self._ring(k) for k in range(1, self.rings)]
-        self.plane = [None] + [self._plane(k) for k in range(1, self.planes)]
+        self.plane = [None] + [self._plane(k % Y * X + k // Y) for k in range(1, self.planes)]
 
     def _ring(self, k):
         z = lax.rem(self.z + k, self.rings)
@@ -153,7 +153,7 @@
 
 
 def kernel(lats, lons, loaded, names, *refs):
-    sources, returned, weight_gradient = refs[:loaded], refs[loaded], refs[loaded + 1]
+    sources, token_sum, weight_gradient = refs[:loaded], refs[loaded], refs[loaded + 1]
     refs = refs[loaded + 2 :]
     targets = refs[:loaded]
     r = types.SimpleNamespace(**dict(zip(names, refs)))
@@ -563,7 +563,7 @@
 
         from_ring[place.z] = part_units[place.z]
 
-    returned_copy = pltpu.make_async_copy(r.returned, returned, r.store_sem.at[0])
+    token_sum_copy = pltpu.make_async_copy(r.token_sum, token_sum, r.store_sem.at[0])
     weight_copy = pltpu.make_async_copy(r.weight_gradient, weight_gradient, r.store_sem.at[1])
 
     def finish_tokens():
@@ -575,8 +575,8 @@
             rows = pl.ds(part_of * half_rows, half_rows)
             inner = back[0:half_rows] if part_of == 0 else r.row_back[...]
             outer = jnp.dot(r.place_sel[...], side_back[part_of], preferred_element_type=F32)
-            r.returned[rows] = (inner.astype(F32) + outer).astype(BF16)
-        returned_copy.start()
+            r.token_sum[rows] = (cot[rows].astype(F32) + (inner.astype(F32) + outer)).astype(BF16)
+        token_sum_copy.start()
 
     def finish_weight():
         ring_part_all.wait_recv()
@@ -589,7 +589,7 @@
         weight_copy.start()
 
     def drain():
-        returned_copy.wait()
+        token_sum_copy.wait()
         weight_copy.wait()
         rows_out.wait_send()
         rows_back.wait_send()
@@ -613,9 +613,17 @@
     join_ring()
     for group in range(groups):
         send_blocks(group)
+    @pl.when(jnp.logical_not(relays.high_end))
+    def _():
+        frame()
+
     forward_arrivals(0)
     forward_arrivals(1)
-    frame()
+
+    @pl.when(relays.high_end)
+    def _():
+        frame()
+
     for group in range(groups):
         collect(group)
         project(group)
@@ -641,7 +649,7 @@
     drain()
 
 
-def finish_kernel(returned, cot, weight, token_grad, weight_gradient, first, second, total, held, load_sem, store_sem):
+def finish_kernel(token_sum, weight, token_grad, weight_gradient, first, held, load_sem, store_sem):
     parts = first.shape[0]
     rows = first.shape[1]
     weight_load = pltpu.make_async_copy(weight, held, store_sem.at[parts])
@@ -652,11 +660,10 @@
         at = pl.ds(i * rows, rows)
         loads.append(
             (
-                pltpu.make_async_copy(returned.at[at], first.at[i], load_sem.at[i, 0]),
-                pltpu.make_async_copy(cot.at[at], second.at[i], load_sem.at[i, 1]),
+                pltpu.make_async_copy(token_sum.at[at], first.at[i], load_sem.at[i, 0]),
             )
         )
-        stores.append(pltpu.make_async_copy(total.at[i], token_grad.at[at], store_sem.at[i]))
+        stores.append(pltpu.make_async_copy(first.at[i], token_grad.at[at], store_sem.at[i]))
     for pair in loads:
         for load in pair:
             load.start()
@@ -665,31 +672,30 @@
     for i in range(parts):
         for load in loads[i]:
             load.wait()
-        total[i] = (second[i].astype(F32) + first[i].astype(F32)).astype(BF16)
         stores[i].start()
     for store in stores:
         store.wait()
     weight_store.wait()
 
 
-def finish(returned, cot, weight):
+def finish(token_sum, weight):
     parts = 3
-    block = VMEM((parts, cot.shape[0] // parts, cot.shape[1]), BF16)
+    block = VMEM((parts, token_sum.shape[0] // parts, token_sum.shape[1]), BF16)
     return pl.pallas_call(
         finish_kernel,
         out_shape=(
-            jax.ShapeDtypeStruct(cot.shape, BF16),
+            jax.ShapeDtypeStruct(token_sum.shape, BF16),
             jax.ShapeDtypeStruct(weight.shape, F32),
         ),
-        in_specs=[pl.BlockSpec(memory_space=pl.ANY)] * 3,
+        in_specs=[pl.BlockSpec(memory_space=pl.ANY)] * 2,
         out_specs=[pl.BlockSpec(memory_space=pl.ANY)] * 2,
         scratch_shapes=[
-            block, block, block, VMEM(weight.shape, F32),
-            pltpu.SemaphoreType.DMA((parts, 2)), pltpu.SemaphoreType.DMA((parts + 2,)),
+            block, VMEM(weight.shape, F32),
+            pltpu.SemaphoreType.DMA((parts, 1)), pltpu.SemaphoreType.DMA((parts + 2,)),
         ],
         compiler_params=pltpu.CompilerParams(vmem_limit_bytes=56 * 2**20),
         name="finish",
-    )(returned, cot, weight)
+    )(token_sum, weight)
 
 
 def frame_tables(cols):
@@ -788,7 +794,7 @@
         side_back=VMEM((2, 32, features), BF16),
         part_units=VMEM((rings, 16, 128), BF16),
         from_ring=VMEM((rings, 16, 128), BF16),
-        returned=VMEM(tok.shape, BF16),
+        token_sum=VMEM(tok.shape, BF16),
         weight_gradient=VMEM(qkv_weight.shape, F32),
         load_sem=dma((len(loaded),)),
         store_sem=dma((2,)),
@@ -804,7 +810,7 @@
     for name, shape in both.items():
         scratch[name + "_send"] = dma(shape)
         scratch[name + "_recv"] = dma(shape)
-    returned, weight_gradient = pl.pallas_call(
+    token_sum, weight_gradient = pl.pallas_call(
         functools.partial(kernel, lats, lons, len(loaded), list(scratch)),
         out_shape=(
             jax.ShapeDtypeStruct(tok.shape, BF16),
@@ -818,7 +824,7 @@
         ),
         name="sub_block",
     )(*loaded.values())
-    token_grad, weight_gradient = finish(returned, cot, weight_gradient)
+    token_grad, weight_gradient = finish(token_sum, weight_gradient)
     return token_grad.reshape(tokens.shape), weight_gradient
 
 

time: 61.1 us -> 60.4 us (0.989)
  the two profiles are of different devices: /device:TPU:6 before, /device:TPU:31 now
where the time goes in v7:
time: 60.4 us; the launch traced here: 60.2 us
  Pallas kernels  59.6 us (99%)
  between operations  0.64 us (1%)
    pallas_call x1, Pallas kernels, on_device(): pl.pallas_call(functools.partial(kernel, lats, lons, len(loaded), list(sc...  57.9 us
    pallas_call x1, Pallas kernels, finish(): pl.pallas_call(finish_kernel, out_shape=(jax.ShapeDtypeStruct(token_sum.s...  1.72 us

profile of v7, /device:TPU:31, one launch (start us, length us, event | category | flops | bytes accessed | tf_op | source)
XLA Modules:
  0.0 60.2 jit_solution(6965634052408120698)
XLA Ops:
  0.6 57.9 %sub_block.1 = (bf16[288,512]{1,0:T(8,128)(2,1)}, f32[8,192]{1,0:T(8,128)}) custom-call(bf16[8,192]{1,0:T(8,128)(2,1)} %refs_0_.1, s32[64]{0:T(128)} %refs_1_.1, bf16[288,512]{1,0:T(8,128)(2,1)} %bitcast.3, bf16[288,512]{1,0:T(8,128)(2,1)} %bitcast.4, bf16[2,48,144]{2,1,0:T(8,128)(2,1)} %constant.16.clone.refs_4_, s32[320,128]{1,0:T(8,128)} %constant.17.clone.refs_5_, ...), custom_call_target="tpu_custom_call" | custom-call | tf_op jit(solution)/shard_map/sub_block/pallas_call | solution.py:813
  58.5 1.7 %finish.1 = (bf16[288,512]{1,0:T(8,128)(2,1)}, f32[8,192]{1,0:T(8,128)}) custom-call(bf16[288,512]{1,0:T(8,128)(2,1)} %get-tuple-element.6.token_sum, f32[8,192]{1,0:T(8,128)} %get-tuple-element.7.weight), custom_call_target="tpu_custom_call" | custom-call | tf_op jit(solution)/shard_map/finish/pallas_call | solution.py:684

commit v8 on v7

--- a/solution.py
+++ b/solution.py
@@ -316,6 +316,8 @@
 
     def send_halos():
         rows_out.start()
+
+    def send_sides():
         corner_out.start()
         side_copy.start()
 
@@ -611,7 +613,9 @@
     send_halos()
     pass_on()
     join_ring()
-    for group in range(groups):
+    send_blocks(0)
+    send_sides()
+    for group in range(1, groups):
         send_blocks(group)
     @pl.when(jnp.logical_not(relays.high_end))
     def _():

time: 60.4 us -> 60.7 us (level)
  the two profiles are of different devices: /device:TPU:31 before, /device:TPU:6 now
where the time goes in v8:
time: 60.7 us; the launch traced here: 60.2 us
  Pallas kernels  59.6 us (98%)
  between operations  0.64 us (1%)
    pallas_call x1, Pallas kernels, on_device(): pl.pallas_call(functools.partial(kernel, lats, lons, len(loaded), list(sc...  57.9 us
    pallas_call x1, Pallas kernels, finish(): pl.pallas_call(finish_kernel, out_shape=(jax.ShapeDtypeStruct(token_sum.s...  1.72 us

profile of v8, /device:TPU:6, one launch (start us, length us, event | category | flops | bytes accessed | tf_op | source)
XLA Modules:
  0.0 60.2 jit_solution(949900158612404818)
XLA Ops:
  0.6 57.9 %sub_block.1 = (bf16[288,512]{1,0:T(8,128)(2,1)}, f32[8,192]{1,0:T(8,128)}) custom-call(bf16[8,192]{1,0:T(8,128)(2,1)} %refs_0_.1, s32[64]{0:T(128)} %refs_1_.1, bf16[288,512]{1,0:T(8,128)(2,1)} %bitcast.3, bf16[288,512]{1,0:T(8,128)(2,1)} %bitcast.4, bf16[2,48,144]{2,1,0:T(8,128)(2,1)} %constant.16.clone.refs_4_, s32[320,128]{1,0:T(8,128)} %constant.17.clone.refs_5_, ...), custom_call_target="tpu_custom_call" | custom-call | tf_op jit(solution)/shard_map/sub_block/pallas_call | solution.py:817
  58.5 1.7 %finish.1 = (bf16[288,512]{1,0:T(8,128)(2,1)}, f32[8,192]{1,0:T(8,128)}) custom-call(bf16[288,512]{1,0:T(8,128)(2,1)} %get-tuple-element.6.token_sum, f32[8,192]{1,0:T(8,128)} %get-tuple-element.7.weight), custom_call_target="tpu_custom_call" | custom-call | tf_op jit(solution)/shard_map/finish/pallas_call | solution.py:688
